TPU v7x, 128 devices: a whole 4x4x4 slice. The times are simulated.
128 devices in a mesh: dev: 128 (over z, y, x, core).
Axes of the slice: x: 4, y: 4, z: 4, core: 2. Of those that a mesh axis runs over, the one named last changes fastest.
Arguments:
- displacement: float32 [3, 524288], P(None, 'dev'), may hold values from -2 to 2
- send_node: int32 [1048576], P('dev'), may hold values from -1 to 4095, as said below
- member_slot: int32 [512, 1024], P('dev'), may hold values from 0 to 8191, as said below
- inverse_part: bfloat16 [512, 1024, 1024], P('dev'), may hold values from -0.09375 to 0.09375
- source_coord: float32 [512, 3, 1024], P('dev'), may hold values from 0 to 1
- target_coord: float32 [512, 3, 1024], P('dev'), may hold values from 0 to 1
- unity_weight: float32 [512, 1024], P('dev'), may hold values from 0.1 to 1
- result_pick: int32 [1048576], P('dev'), may hold values from -1 to 4095, as said below
- receive_vertex: int32 [1048576], P('dev'), may hold values from 0 to 8191
- mesh_before: float32 [3, 2048, 96, 512], P(None, 'dev'), may hold values from -6 to 6
Outputs:
- mesh_motion: float32 [3, 2048, 96, 512], P(None, 'dev')
Inputs may be any that keep to these rules, and one draw needn't show every extreme that they name: `send_node`: each device's entries form 128 blocks of 64, block e for cluster owner e; in each block the live entries (0 or more) come first and -1 fills the rest; each block has at least one live entry and each device has one block with all 64 live. `member_slot`: every entry names a live slot of send_node sent to the cluster's owner. `result_pick`: each device's entries form 128 blocks of 64, block e for fluid owner e; in each block the live entries (0 or more) come first and -1 fills the rest; each block has at least one live entry and each device has one block with all 64 live.
All inputs are finite; a program needn't handle non-finite values.
Results may differ from a plain program's by a relative error of at most 0.00043.
Values sent between devices are 32-bit elements; how exact they have to be, the bound alone decides.
A program may use at most 128 MiB of HBM per device.

v0:
```python
import jax
import jax.numpy as jnp
from jax import lax
from jax.sharding import PartitionSpec as P

relax_rate = 0.8
kernel_sharpness = 8.0


def extended_2(cells, sides, width):
    for axis, dim in sides:
        count = lax.axis_size(axis)
        ends = count - 1
        head = lax.slice_in_dim(cells, 0, width, axis=dim)
        tail = lax.slice_in_dim(cells, cells.shape[dim] - width, cells.shape[dim], axis=dim)
        cells = jnp.concatenate(
            [
                lax.ppermute(tail, axis, [(i, (i + 1) % count) for i in range(ends)]),
                cells,
                lax.ppermute(head, axis, [((i + 1) % count, i) for i in range(ends)]),
            ],
            axis=dim,
        )
    return cells


def relax(extended):
    center = extended[:, 1:-1]
    padded = jnp.pad(center, ((0, 0), (0, 0), (1, 1), (1, 1)))
    beside = extended[:, 2:] + extended[:, :-2]
    beside = beside + padded[:, :, 2:, 1:-1] + padded[:, :, :-2, 1:-1]
    beside = beside + padded[:, :, 1:-1, 2:] + padded[:, :, 1:-1, :-2]
    moved = center + relax_rate * (beside * (1.0 / 6.0) - center)
    yrows = lax.broadcasted_iota(jnp.int32, center.shape, 2)
    return jnp.where(yrows == 0, center, moved)


def sweep(field):
    extended = extended_2(field, (("dev", 1),), 1)
    return relax(extended)


def local(
    displacement,
    send_node,
    member_slot,
    inverse_part,
    source_coord,
    target_coord,
    unity_weight,
    result_pick,
    receive_vertex,
    mesh_before,
):
    device_count = lax.axis_size("dev")
    slot_cap = send_node.shape[0] // device_count
    picked = jnp.take(displacement, jnp.maximum(send_node, 0), axis=1)
    outgoing = jnp.where(send_node[None, :] >= 0, picked, 0.0).reshape(3, device_count, slot_cap)
    arrived = lax.all_to_all(outgoing, "dev", split_axis=1, concat_axis=1, tiled=True).reshape(
        3, device_count * slot_cap
    )
    members = jnp.take(arrived, member_slot, axis=1)
    coupling = jnp.einsum(
        "kcp,cqp->kcq",
        members.astype(jnp.bfloat16),
        inverse_part,
        preferred_element_type=jnp.float32,
    )
    coefficient = members + coupling
    gap = target_coord[:, 0, :, None] - source_coord[:, 0, None, :]
    spread = gap * gap
    gap = target_coord[:, 1, :, None] - source_coord[:, 1, None, :]
    spread = spread + gap * gap
    gap = target_coord[:, 2, :, None] - source_coord[:, 2, None, :]
    spread = spread + gap * gap
    kernel = jnp.exp(-kernel_sharpness * spread)
    contrib = jnp.einsum(
        "kcp,ctp->kct",
        coefficient,
        kernel,
        precision=lax.Precision.HIGHEST,
        preferred_element_type=jnp.float32,
    )
    contrib = contrib * unity_weight[None]
    flat_results = contrib.reshape(3, -1)
    result_cap = result_pick.shape[0] // device_count
    taken = jnp.take(flat_results, jnp.maximum(result_pick, 0), axis=1)
    outgoing_results = jnp.where(result_pick[None, :] >= 0, taken, 0.0).reshape(
        3, device_count, result_cap
    )
    returned = lax.all_to_all(
        outgoing_results, "dev", split_axis=1, concat_axis=1, tiled=True
    ).reshape(3, device_count * result_cap)
    width_x = mesh_before.shape[1]
    depth_z = mesh_before.shape[3]
    interface = jnp.zeros((3, width_x * depth_z), jnp.float32).at[:, receive_vertex].add(returned)
    yrows = lax.broadcasted_iota(jnp.int32, mesh_before.shape, 2)
    start_field = jnp.where(yrows == 0, interface.reshape(3, width_x, 1, depth_z), mesh_before)
    return sweep(sweep(start_field))


def solution(mesh):
    in_specs = (
        P(None, "dev"),
        P("dev"),
        P("dev", None),
        P("dev", None, None),
        P("dev", None, None),
        P("dev", None, None),
        P("dev", None),
        P("dev"),
        P("dev"),
        P(None, "dev", None, None),
    )
    out_specs = P(None, "dev", None, None)
    return jax.shard_map(local, mesh=mesh, in_specs=in_specs, out_specs=out_specs, check_vma=False)
```

profile of v0, /device:TPU:32, one launch (start us, length us, event | category | flops | bytes accessed | tf_op | source)
XLA Modules:
  0.0 319.6 jit_solution(11551722511432730149)
XLA Ops:
  0.0 0.0 copy-start.1
  0.0 0.0 copy-start.2
  0.0 0.0 copy-start.5
  0.0 0.0 copy-start.4
  0.0 0.0 copy-start.3
  0.0 0.8 broadcast_compare_fusion
  0.9 0.8 maximum_clamp_fusion.1
  1.6 1.5 copy.24
  3.1 28.0 %gather_fusion.1 = f32[8192,3]{1,0:T(8,128)} fusion(f32[3,4096]{0,1:T(8,128)S(1)} %copy.24, s32[8192]{0:T(1024)S(1)} %maximum_clamp_fusion.1), kind=kCustom, calls=%fused_computation.clone | custom fusion | bytes 229376 | tf_op jit(solution)/shard_map/jit(_take)/gather | solution.py:57
  31.1 7.6 %bitcast_select_fusion.1 = f32[3,8192]{0,1:T(8,128)} fusion(f32[8192,3]{1,0:T(8,128)} %gather_fusion.1, pred[8192]{0:T(1024)(128)(4,1)S(1)} %get-tuple-element.19, pred[8192]{0:T(1024)(128)(4,1)S(1)} %get-tuple-element.18), kind=kLoop, calls=%fused_computation.54 | loop fusion | flops 49152 | bytes 212992 | tf_op jit(solution)/shard_map/jit(_where)/select_n | solution.py:58
  38.7 3.0 copy.25
  41.7 0.0 copy-start.6
  41.7 0.9 reshape.83
  42.6 10.2 %all-to-all-start = ((f32[128,1,192]{2,1,0:T(1,128)}), f32[128,1,192]{2,1,0:T(1,128)S(1)}, u32[]{:S(2)}, u32[]{:S(2)}) async-start(f32[128,1,192]{2,1,0:T(1,128)} %reshape.83), calls=%async_computation | async-start | bytes 262144 | tf_op jit(solution)/shard_map/all_to_all | solution.py:59
  52.8 0.0 copy-done.1
  52.9 0.0 copy-done.2
  52.9 0.0 copy-done.5
  52.9 0.0 copy-done.4
  52.9 0.0 copy-done.3
  53.0 8.9 %all-to-all-done = f32[128,1,192]{2,1,0:T(1,128)S(1)} async-done(((f32[128,1,192]{2,1,0:T(1,128)}), f32[128,1,192]{2,1,0:T(1,128)S(1)}, u32[]{:S(2)}, u32[]{:S(2)}) %all-to-all-start) | async-done | bytes 98336 | tf_op jit(solution)/shard_map/all_to_all | solution.py:59
  61.9 0.6 broadcast.88
  62.4 0.9 reduce
  63.4 0.1 reshape.84
  63.5 2.7 copy.26
  66.3 13.0 %gather_fusion = f32[4096,3]{1,0:T(8,128)S(1)} fusion(f32[3,8192]{0,1:T(8,128)} %bitcast.46, s32[4096]{0:T(1024)S(1)} %bitcast_clamp_fusion), kind=kCustom, calls=%fused_computation.2 | custom fusion | bytes 114688 | tf_op jit(solution)/shard_map/jit(_take)/gather | solution.py:62
  79.2 0.6 copy.28
  79.8 5.7 %fusion.36 = f32[3,4,1024]{2,0,1:T(4,128)S(1)} fusion(bf16[4,1024,1024]{2,1,0:T(8,128)(2,1)} %param.15, f32[4,1024,3]{1,2,0:T(4,128)S(1)} %copy.28, pred[4,1024]{1,0:T(4,128)(4,1)S(1)} %compare_and_fusion), kind=kOutput, calls=%fused_computation.58 | convolution fusion | flops 25214976 | bytes 8491008 | tf_op jit(solution)/shard_map/kcp,cqp->kcq/dot_general | solution.py:63
  85.5 0.0 copy-done.6
  85.5 20.8 %fusion.37 = f32[4,1024,3]{1,2,0:T(4,128)S(1)} fusion(f32[3,4,1024]{2,0,1:T(4,128)S(1)} %fusion.36, f32[4,1024]{1,0:T(4,128)S(1)} %get-tuple-element.14, f32[4,1024]{1,0:T(4,128)S(1)} %get-tuple-element.21, f32[4,1024]{1,0:T(4,128)S(1)} %get-tuple-element.15, f32[4,1024]{1,0:T(4,128)S(1)} %get-tuple-element.20, f32[4,1024]{1,0:T(4,128)S(1)} %get-tuple-element.13, ...), kind=kOutput, calls=%fused_computation.59 | convolution fusion | flops 188755968 | bytes 212992 | tf_op jit(solution)/shard_map/kcp,ctp->kct/dot_general | solution.py:77
  106.3 0.7 copy.29
  107.0 28.0 %gather_fusion.2 = f32[8192,3]{1,0:T(8,128)} fusion(f32[3,4096]{0,1:T(8,128)S(1)} %copy.29, s32[8192]{0:T(1024)S(1)} %maximum_clamp_fusion), kind=kCustom, calls=%fused_computation.1.clone | custom fusion | bytes 229376 | tf_op jit(solution)/shard_map/jit(_take)/gather | solution.py:87
  135.0 7.6 %bitcast_select_fusion = f32[3,8192]{0,1:T(8,128)} fusion(f32[8192,3]{1,0:T(8,128)} %gather_fusion.2, pred[8192]{0:T(1024)(128)(4,1)S(1)} %get-tuple-element.17, pred[8192]{0:T(1024)(128)(4,1)S(1)} %get-tuple-element.16), kind=kLoop, calls=%fused_computation.53 | loop fusion | flops 49152 | bytes 212992 | tf_op jit(solution)/shard_map/jit(_where)/select_n | solution.py:88
  142.6 3.0 copy.30
  145.6 0.9 reshape.85
  146.5 5.2 %all-to-all-start.1 = ((f32[128,1,192]{2,1,0:T(1,128)}), f32[128,1,192]{2,1,0:T(1,128)S(1)}, u32[]{:S(2)}, u32[]{:S(2)}) async-start(f32[128,1,192]{2,1,0:T(1,128)} %reshape.85), calls=%async_computation.1 | async-start | bytes 262144 | tf_op jit(solution)/shard_map/all_to_all | solution.py:91
  151.7 9.0 %all-to-all-done.1 = f32[128,1,192]{2,1,0:T(1,128)S(1)} async-done(((f32[128,1,192]{2,1,0:T(1,128)}), f32[128,1,192]{2,1,0:T(1,128)S(1)}, u32[]{:S(2)}, u32[]{:S(2)}) %all-to-all-start.1) | async-done | bytes 98336 | tf_op jit(solution)/shard_map/all_to_all | solution.py:91
  160.7 0.9 reduce.1
  161.7 0.1 reshape.86
  161.8 0.1 reshape.65
  161.9 2.7 copy.32
  164.6 46.5 %scatter_custom_fusion = f32[3,8192]{0,1:T(8,128)} fusion(s32[8192]{0:T(1024)S(1)} %compare_select_fusion, f32[8192,3]{1,0:T(8,128)} %copy.32, f32[]{:T(128)} %constant.8.clone.1), kind=kCustom, calls=%fused_computation.55 | custom fusion | flops 24576 | bytes 98816 | tf_op jit(solution)/shard_map/scatter-add | solution.py:96
  211.1 2.8 copy.33
  214.0 5.2 %broadcast_select_fusion = f32[3,16,96,512]{3,2,1,0:T(8,128)S(1)} fusion(f32[3,16,96,512]{3,2,1,0:T(8,128)} %param.21, f32[3,16,512]{2,1,0:T(8,128)S(1)} %copy.33, pred[96]{0:T(512)(128)(4,1)S(1)} %iota_compare_fusion), kind=kLoop, calls=%fused_computation.52 | loop fusion | flops 2359296 | bytes 18972768 | tf_op jit(solution)/shard_map/jit(_where)/select_n | solution.py:98
  219.2 0.0 copy-start
  219.2 3.7 %copy-done = f32[3,16,96,512]{3,2,1,0:T(8,128)} copy-done((f32[3,16,96,512]{3,2,1,0:T(8,128)}, f32[3,16,96,512]{3,2,1,0:T(8,128)S(1)}, u32[]{:S(2)}) %copy-start) | copy-done | bytes 9437208
  222.9 0.1 fusion.47
  223.1 4.1 %collective-permute-start = (f32[3,1,96,512]{3,2,1,0:T(8,128)S(1)}, f32[3,1,96,512]{3,2,1,0:T(8,128)S(1)}, u32[]{:S(2)}, u32[]{:S(2)}) collective-permute-start(f32[3,1,96,512]{3,2,1,0:T(8,128)S(1)} %get-tuple-element.8), channel_id=1, source_target_pairs={{1,0},{2,1},{3,2},{4,3},{5,4},{6,5},{7,6},{8,7},{9,8},{10,9},{11,1... | collective-permute-start | bytes 1769480 | tf_op jit(solution)/shard_map/ppermute | solution.py:20
  227.2 1.9 collective-permute-start.1
  229.1 5.5 %collective-permute-done = f32[3,1,96,512]{3,2,1,0:T(8,128)S(1)} collective-permute-done((f32[3,1,96,512]{3,2,1,0:T(8,128)S(1)}, f32[3,1,96,512]{3,2,1,0:T(8,128)S(1)}, u32[]{:S(2)}, u32[]{:S(2)}) %collective-permute-start) | collective-permute-done | bytes 589856 | tf_op jit(solution)/shard_map/ppermute | solution.py:20
  234.6 8.0 %collective-permute-done.1 = f32[3,1,96,512]{3,2,1,0:T(8,128)S(1)} collective-permute-done((f32[3,1,96,512]{3,2,1,0:T(8,128)S(1)}, f32[3,1,96,512]{3,2,1,0:T(8,128)S(1)}, u32[]{:S(2)}, u32[]{:S(2)}) %collective-permute-start.1) | collective-permute-done | bytes 589856 | tf_op jit(solution)/shard_map/ppermute | solution.py:18
  242.6 29.3 %add_select_fusion.1 = f32[3,16,96,512]{3,2,1,0:T(8,128)} fusion(f32[3,16,96,512]{3,2,1,0:T(8,128)} %copy-done, f32[3,1,96,512]{3,2,1,0:T(8,128)S(1)} %collective-permute-done.1, f32[3,1,96,512]{3,2,1,0:T(8,128)S(1)} %collective-permute-done, pred[96]{0:T(512)(128)(4,1)S(1)} %iota_compare_fusion), kind=kLoop, calls=%fused_computation.24 | loop fusion | flops 28311552 | bytes 20054112 | tf_op jit(solution)/shard_map/jit(_where)/select_n | solution.py:35
  271.9 1.4 fusion.46
  273.3 1.9 collective-permute-start.2
  275.2 2.4 collective-permute-start.3
  277.6 5.0 %collective-permute-done.2 = f32[3,1,96,512]{3,2,1,0:T(8,128)S(1)} collective-permute-done((f32[3,1,96,512]{3,2,1,0:T(8,128)S(1)}, f32[3,1,96,512]{3,2,1,0:T(8,128)S(1)}, u32[]{:S(2)}, u32[]{:S(2)}) %collective-permute-start.2) | collective-permute-done | bytes 589856 | tf_op jit(solution)/shard_map/ppermute | solution.py:20
  282.6 8.0 %collective-permute-done.3 = f32[3,1,96,512]{3,2,1,0:T(8,128)S(1)} collective-permute-done((f32[3,1,96,512]{3,2,1,0:T(8,128)S(1)}, f32[3,1,96,512]{3,2,1,0:T(8,128)S(1)}, u32[]{:S(2)}, u32[]{:S(2)}) %collective-permute-start.3) | collective-permute-done | bytes 589856 | tf_op jit(solution)/shard_map/ppermute | solution.py:18
  290.6 29.0 %add_select_fusion = f32[3,16,96,512]{3,2,1,0:T(8,128)} fusion(f32[3,16,96,512]{3,2,1,0:T(8,128)} %add_select_fusion.1, f32[3,1,96,512]{3,2,1,0:T(8,128)S(1)} %collective-permute-done.3, f32[3,1,96,512]{3,2,1,0:T(8,128)S(1)} %collective-permute-done.2, pred[96]{0:T(512)(128)(4,1)S(1)} %iota_compare_fusion), kind=kLoop, calls=%fused_computation.23 | loop fusion | flops 28311552 | bytes 20054112 | tf_op jit(solution)/shard_map/jit(_where)/select_n | solution.py:35
  (9 shorter events, 0.1 us)
Async XLA Ops:
  0.0 52.8 %copy-start.1 = (s32[8192]{0:T(1024)S(1)}, s32[8192]{0:T(1024)}, u32[]{:S(2)}) copy-start(s32[8192]{0:T(1024)} %param.19) | copy-start | bytes 98308
  0.0 52.9 %copy-start.2 = (s32[4,1024]{1,0:T(4,128)S(1)}, s32[4,1024]{1,0:T(4,128)}, u32[]{:S(2)}) copy-start(s32[4,1024]{1,0:T(4,128)} %param.14) | copy-start | bytes 49156
  0.0 52.9 %copy-start.5 = (s32[8192]{0:T(1024)S(1)}, s32[8192]{0:T(1024)}, u32[]{:S(2)}) copy-start(s32[8192]{0:T(1024)} %param.20) | copy-start | bytes 98308
  0.0 52.9 %copy-start.4 = (f32[4,3,1024]{2,0,1:T(4,128)S(1)}, f32[4,3,1024]{2,0,1:T(4,128)}, u32[]{:S(2)}) copy-start(f32[4,3,1024]{2,0,1:T(4,128)} %param.17) | copy-start | bytes 147460
  0.0 52.9 %copy-start.3 = (f32[4,3,1024]{2,0,1:T(4,128)S(1)}, f32[4,3,1024]{2,0,1:T(4,128)}, u32[]{:S(2)}) copy-start(f32[4,3,1024]{2,0,1:T(4,128)} %param.16) | copy-start | bytes 147460
  41.7 43.8 %copy-start.6 = (f32[4,1024]{1,0:T(4,128)S(1)}, f32[4,1024]{1,0:T(4,128)}, u32[]{:S(2)}) copy-start(f32[4,1024]{1,0:T(4,128)} %param.18) | copy-start | bytes 49156
  42.6 19.3 %all-to-all-start = ((f32[128,1,192]{2,1,0:T(1,128)}), f32[128,1,192]{2,1,0:T(1,128)S(1)}, u32[]{:S(2)}, u32[]{:S(2)}) async-start(f32[128,1,192]{2,1,0:T(1,128)} %reshape.83), calls=%async_computation | async-start | bytes 262144 | tf_op jit(solution)/shard_map/all_to_all | solution.py:59
  146.5 14.2 %all-to-all-start.1 = ((f32[128,1,192]{2,1,0:T(1,128)}), f32[128,1,192]{2,1,0:T(1,128)S(1)}, u32[]{:S(2)}, u32[]{:S(2)}) async-start(f32[128,1,192]{2,1,0:T(1,128)} %reshape.85), calls=%async_computation.1 | async-start | bytes 262144 | tf_op jit(solution)/shard_map/all_to_all | solution.py:91
  219.2 3.7 %copy-start = (f32[3,16,96,512]{3,2,1,0:T(8,128)}, f32[3,16,96,512]{3,2,1,0:T(8,128)S(1)}, u32[]{:S(2)}) copy-start(f32[3,16,96,512]{3,2,1,0:T(8,128)S(1)} %broadcast_select_fusion) | copy-start | bytes 28311556
  223.1 11.5 %collective-permute-start = (f32[3,1,96,512]{3,2,1,0:T(8,128)S(1)}, f32[3,1,96,512]{3,2,1,0:T(8,128)S(1)}, u32[]{:S(2)}, u32[]{:S(2)}) collective-permute-start(f32[3,1,96,512]{3,2,1,0:T(8,128)S(1)} %get-tuple-element.8), channel_id=1, source_target_pairs={{1,0},{2,1},{3,2},{4,3},{5,4},{6,5},{7,6},{8,7},{9,8},{10,9},{11,1... | collective-permute-start | bytes 1769480 | tf_op jit(solution)/shard_map/ppermute | solution.py:20
  227.2 15.4 %collective-permute-start.1 = (f32[3,1,96,512]{3,2,1,0:T(8,128)S(1)}, f32[3,1,96,512]{3,2,1,0:T(8,128)S(1)}, u32[]{:S(2)}, u32[]{:S(2)}) collective-permute-start(f32[3,1,96,512]{3,2,1,0:T(8,128)S(1)} %get-tuple-element.9), channel_id=1, source_target_pairs={{0,1},{1,2},{2,3},{3,4},{4,5},{5,6},{6,7},{7,8},{8,9},{9,10},{10,1... | collective-permute-start | bytes 1769480 | tf_op jit(solution)/shard_map/ppermute | solution.py:18
  273.3 9.3 %collective-permute-start.2 = (f32[3,1,96,512]{3,2,1,0:T(8,128)S(1)}, f32[3,1,96,512]{3,2,1,0:T(8,128)S(1)}, u32[]{:S(2)}, u32[]{:S(2)}) collective-permute-start(f32[3,1,96,512]{3,2,1,0:T(8,128)S(1)} %get-tuple-element.6), channel_id=1, source_target_pairs={{1,0},{2,1},{3,2},{4,3},{5,4},{6,5},{7,6},{8,7},{9,8},{10,9},{11,1... | collective-permute-start | bytes 1769480 | tf_op jit(solution)/shard_map/ppermute | solution.py:20
  275.2 15.4 %collective-permute-start.3 = (f32[3,1,96,512]{3,2,1,0:T(8,128)S(1)}, f32[3,1,96,512]{3,2,1,0:T(8,128)S(1)}, u32[]{:S(2)}, u32[]{:S(2)}) collective-permute-start(f32[3,1,96,512]{3,2,1,0:T(8,128)S(1)} %get-tuple-element.7), channel_id=1, source_target_pairs={{0,1},{1,2},{2,3},{3,4},{4,5},{5,6},{6,7},{7,8},{8,9},{9,10},{10,1... | collective-permute-start | bytes 1769480 | tf_op jit(solution)/shard_map/ppermute | solution.py:18
where the time goes:
time: 320 us
  other arithmetic  129 us (40%)
  local copies, waits for them, and re-layouts  93.9 us (29%)
  waiting for transfers between devices  44.4 us (14%)
  matrix products  26.5 us (8%)
  starting transfers between devices  25.8 us (8%)
    select_n x2, other arithmetic, relax(): return jnp.where(yrows == 0, center, moved)  58.2 us
    scatter-add x1, other arithmetic, local(): jnp.zeros((3, width_x * depth_z), jnp.float32).at[:, receive_vertex]  46.5 us
    gather x1, local copies, waits for them, and re-layouts, local(): picked = jnp.take(displacement, jnp.maximum(send_node, 0), axis=1)  28 us
    gather x1, local copies, waits for them, and re-layouts, local(): taken = jnp.take(flat_results, jnp.maximum(result_pick, 0), axis=1)  28 us
    dot_general x1, matrix products, local(): jnp.einsum('kcp,ctp->kct', coefficient, kernel, precision=lax.Precision.H...  20.8 us
    ppermute x2, waiting for transfers between devices, extended_2(): lax.ppermute(tail, axis, [(i, (i + 1) % count) for i in range(ends)])  16.1 us
    gather x2, local copies, waits for them, and re-layouts, local(): members = jnp.take(arrived, member_slot, axis=1)  13.6 us
    ppermute x2, waiting for transfers between devices, extended_2(): lax.ppermute(head, axis, [((i + 1) % count, i) for i in range(ends)])  10.4 us
  transfers between devices with their start and end apart: 6, of which 6 were waited for; matrix products, arithmetic and copies ran while one was open for 0% of the time, Pallas kernels for 0%

commit v1 on v0

v1 whole, which is shorter than its diff:
```python
import functools

import jax
import jax.numpy as jnp
from jax import lax
from jax.experimental import pallas as pl
from jax.experimental.pallas import tpu as pltpu
from jax.sharding import PartitionSpec as P

relax_rate = 0.8
kernel_sharpness = 8.0
log2_e = 1.4426950408889634
spread_rate = relax_rate / 6.0
keep_rate = 1.0 - relax_rate

MESH = pl.DeviceIdType.MESH
f32 = jnp.float32
bf16 = jnp.bfloat16


def vmem():
    return pl.BlockSpec(memory_space=pltpu.VMEM)


def lookup(row, lanes):
    spread = jnp.broadcast_to(row, lanes.shape)
    return jnp.take_along_axis(spread, lanes, axis=1, mode="promise_in_bounds")


def message_index(index_ref, step):
    x, core = step // 2, step % 2
    even = index_ref[pl.ds(x, 8, stride=8), :]
    odd = index_ref[pl.ds(4 + x, 8, stride=8), :]
    lane = lax.broadcasted_iota(jnp.int32, (8, 128), 1)
    if core == 0:
        return jnp.where(lane < 64, even, pltpu.roll(odd, 64, 1))
    return jnp.where(lane < 64, pltpu.roll(even, 64, 1), odd)


def pick_messages(index_ref, row_of, out_ref):
    for half in range(2):
        index = [message_index(index_ref, 4 * half + g) for g in range(4)]
        high = [jnp.right_shift(i, 7) for i in index]
        low = [jnp.bitwise_and(i, 127) for i in index]
        total = [[jnp.zeros((8, 128), f32) for _ in range(3)] for _ in range(4)]
        for r in range(32):
            hit = [h == r for h in high]
            for k in range(3):
                row = row_of(k, r)
                for g in range(4):
                    total[g][k] = jnp.where(hit[g], lookup(row, low[g]), total[g][k])
        for g in range(4):
            for k in range(3):
                out_ref[(4 * half + g) * 3 + k] = total[g][k]


def send_kernel(disp_ref, node_ref, out_ref):
    pick_messages(
        node_ref, lambda k, r: disp_ref[k : k + 1, r * 128 : (r + 1) * 128], out_ref
    )


def exchange_kernel(y_ref, t_ref, held, ready, landed, send1, recv1, send2, recv2):
    me = lax.axis_index("dev")
    outer, inner = me // 8, me % 8

    barrier = pltpu.get_barrier_semaphore()
    for i in range(1, 8):
        peer = outer * 8 + (inner + i) % 8
        pl.semaphore_signal(barrier, inc=1, device_id=(peer,), device_id_type=MESH)
    for i in range(1, 16):
        peer = ((outer + i) % 16) * 8 + inner
        pl.semaphore_signal(barrier, inc=1, device_id=(peer,), device_id_type=MESH)
    pl.semaphore_wait(barrier, 22)

    copies = []
    for i in range(1, 8):
        p = (inner + i) % 8
        copies.append(
            pltpu.make_async_remote_copy(
                src_ref=y_ref.at[pl.ds(pl.multiple_of(p * 24, 8), 24)],
                dst_ref=held.at[pl.ds(pl.multiple_of(inner * 24, 8), 24)],
                send_sem=send1.at[i - 1],
                recv_sem=recv1.at[i - 1],
                device_id=(outer * 8 + p,),
                device_id_type=MESH,
            )
        )
        copies[-1].start()
    mine = pl.ds(pl.multiple_of(inner * 24, 8), 24)
    held[mine, :] = y_ref[mine, :]
    for copy in copies:
        copy.wait()

    lane = lax.broadcasted_iota(jnp.int32, (4, 128), 1)
    for m in range(8):
        for k in range(3):
            first = held[pl.ds(k * 8 + m, 4, stride=48), :]
            second = held[pl.ds(24 + k * 8 + m, 4, stride=48), :]
            ready[2 * m, 4 * k : 4 * k + 4, :] = jnp.where(
                lane < 64, first, pltpu.roll(second, 64, 1)
            )
            ready[2 * m + 1, 4 * k : 4 * k + 4, :] = jnp.where(
                lane < 64, pltpu.roll(first, 64, 1), second
            )

    copies = []
    for i in range(1, 16):
        p = (outer + i) % 16
        copies.append(
            pltpu.make_async_remote_copy(
                src_ref=ready.at[p],
                dst_ref=landed.at[outer],
                send_sem=send2.at[i - 1],
                recv_sem=recv2.at[i - 1],
                device_id=(p * 8 + inner,),
                device_id_type=MESH,
            )
        )
        copies[-1].start()
    landed[outer] = ready[outer]
    for copy in copies:
        copy.wait()
    t_ref[...] = landed[...]


def exchange(messages, collective_id):
    return pl.pallas_call(
        exchange_kernel,
        out_shape=jax.ShapeDtypeStruct((16, 12, 128), f32),
        in_specs=[vmem()],
        out_specs=vmem(),
        scratch_shapes=[
            pltpu.VMEM((192, 128), f32),
            pltpu.VMEM((16, 12, 128), f32),
            pltpu.VMEM((16, 12, 128), f32),
            pltpu.SemaphoreType.DMA((7,)),
            pltpu.SemaphoreType.DMA((7,)),
            pltpu.SemaphoreType.DMA((15,)),
            pltpu.SemaphoreType.DMA((15,)),
        ],
        compiler_params=pltpu.CompilerParams(
            collective_id=collective_id, has_side_effects=True
        ),
    )(messages.reshape(192, 128))


def three_parts(value):
    high = value.astype(bf16).astype(f32)
    rest = value - high
    middle = rest.astype(bf16).astype(f32)
    return high, middle, rest - middle


def cluster_rows(ref, c, rows):
    return jnp.concatenate([ref[q, pl.ds(c, rows, stride=4), :] for q in range(8)], axis=1)


def cluster_kernel(
    t_ref, slot_ref, inv_hbm, source_ref, target_ref, weight_ref, pick_ref, out_ref,
    inv, loaded, member, left, right, result,
):
    for c in range(4):
        pltpu.make_async_copy(inv_hbm.at[c], inv.at[c], loaded.at[c]).start()

    left[...] = jnp.zeros_like(left)
    right[...] = jnp.zeros_like(right)
    ones = jnp.ones((4, 1024), f32)
    row = 0
    source_norm = jnp.zeros((4, 1024), f32)
    target_norm = jnp.zeros((4, 1024), f32)

    def put(a, b):
        nonlocal row
        for q in range(8):
            left[q, 4 * row : 4 * row + 4, :] = a[:, 128 * q : 128 * (q + 1)]
            right[q, 4 * row : 4 * row + 4, :] = b[:, 128 * q : 128 * (q + 1)]
        row += 1

    for d in range(3):
        s = source_ref[d]
        t = target_ref[d]
        source_norm += s * s
        target_norm += t * t
        sh, sm, sl = three_parts(s)
        th, tm, tl = three_parts(t * (2.0 * kernel_sharpness * log2_e))
        for a, b in ((sh, th), (sh, tm), (sm, th), (sh, tl), (sl, th), (sm, tm)):
            put(a, b)
    for part in three_parts(source_norm * (-kernel_sharpness * log2_e)):
        put(part, ones)
    for part in three_parts(target_norm * (-kernel_sharpness * log2_e)):
        put(ones, part)

    member[...] = jnp.zeros_like(member)
    index = [
        jnp.concatenate(
            [slot_ref[:, 256 * m : 256 * m + 128], slot_ref[:, 256 * m + 128 : 256 * m + 256]],
            axis=0,
        )
        for m in range(4)
    ]
    high = [jnp.right_shift(i, 7) for i in index]
    low = [jnp.bitwise_and(i, 127) for i in index]

    def gather(zy, total):
        total = list(total)
        for j in range(4):
            hit = [h == zy * 4 + j for h in high]
            for k in range(3):
                line = t_ref[zy, 4 * k + j : 4 * k + j + 1, :]
                for m in range(4):
                    total[3 * m + k] = jnp.where(hit[m], lookup(line, low[m]), total[3 * m + k])
        return tuple(total)

    total = lax.fori_loop(
        0, 16, gather, tuple(jnp.zeros((8, 128), f32) for _ in range(12))
    )
    for m in range(4):
        for k in range(3):
            value = total[3 * m + k]
            member[2 * m, 4 * k : 4 * k + 4, :] = value[0:4]
            member[2 * m + 1, 4 * k : 4 * k + 4, :] = value[4:8]

    for c in range(4):
        members = cluster_rows(member, c, 8)
        padded = jnp.concatenate([members, jnp.zeros((8, 1024), f32)], axis=0)
        pltpu.make_async_copy(inv_hbm.at[c], inv.at[c], loaded.at[c]).wait()
        coupling = lax.dot_general(
            padded.astype(bf16), inv[c], (((1,), (1,)), ((), ())), preferred_element_type=f32
        )
        coefficient = members + coupling[0:8]
        upper = coefficient.astype(bf16).astype(f32)
        both = jnp.concatenate([upper, coefficient - upper], axis=0).astype(bf16)

        source_rows = cluster_rows(left, c, 32).T.astype(bf16)
        target_rows = cluster_rows(right, c, 32).astype(bf16)
        summed = jnp.zeros((16, 1024), f32)
        for p in range(4):
            exponent = jnp.dot(
                source_rows[256 * p : 256 * (p + 1)], target_rows, preferred_element_type=f32
            )
            kernel = jnp.exp2(exponent)
            kernel_high = kernel.astype(bf16)
            kernel_low = (kernel - kernel_high.astype(f32)).astype(bf16)
            part = both[:, 256 * p : 256 * (p + 1)]
            summed += jnp.dot(part, kernel_high, preferred_element_type=f32)
            summed += jnp.dot(part, kernel_low, preferred_element_type=f32)
        result[c] = (summed[0:8] + summed[8:16]) * weight_ref[c : c + 1, :]

    pick_messages(
        pick_ref,
        lambda k, r: result[r // 8, k : k + 1, (r % 8) * 128 : (r % 8 + 1) * 128],
        out_ref,
    )


def scatter_kernel(t_ref, vertex_ref, out_ref, values, places, total):
    def chunk(zy, carry):
        for j in range(4):
            vertex = vertex_ref[pl.ds(zy * 4 + j, 1), :]
            high = jnp.broadcast_to(jnp.right_shift(vertex, 7), (64, 128))
            low = jnp.broadcast_to(jnp.bitwise_and(vertex, 127), (128, 128))
            at_high = high == lax.broadcasted_iota(jnp.int32, (64, 128), 0)
            at_low = low == lax.broadcasted_iota(jnp.int32, (128, 128), 0)
            lanes = slice(128 * j, 128 * j + 128)
            places[:, lanes] = jnp.where(at_low, 1.0, 0.0).astype(bf16)
            for k in range(3):
                value = t_ref[zy, 4 * k + j : 4 * k + j + 1, :]
                for s, part in enumerate(three_parts(value)):
                    spread = jnp.broadcast_to(part, (64, 128))
                    top = (3 * k + s) * 64
                    values[top : top + 64, lanes] = jnp.where(at_high, spread, 0.0).astype(bf16)
        product = lax.dot_general(
            values[...], places[...], (((1,), (1,)), ((), ())), preferred_element_type=f32
        )
        total[...] += product
        return carry

    total[...] = jnp.zeros_like(total)
    lax.fori_loop(0, 16, chunk, 0)
    for k in range(3):
        top = 3 * k * 64
        for q in range(4):
            out_ref[k, :, 128 * q : 128 * (q + 1)] = (
                total[pl.ds(top + q, 16, stride=4), :]
                + total[pl.ds(top + 64 + q, 16, stride=4), :]
                + total[pl.ds(top + 128 + q, 16, stride=4), :]
            )


def swept(ref, out_ref, source, target, wall, scale=None):
    before, after = source - 1, source + 1
    rows = 16
    lane = lax.broadcasted_iota(jnp.int32, (rows, 512), 1)
    line = lax.broadcasted_iota(jnp.int32, (rows, 512), 0)
    for y in range(0, 96, rows):
        center = ref[source, y : y + rows, :]
        if y == 0:
            if wall:
                center = jnp.where(line == 0, 0.0, center)
            above = pltpu.roll(center, 1, 0)
        else:
            above = ref[source, y - 1 : y - 1 + rows, :]
        if y + rows == 96:
            below = jnp.where(line == rows - 1, 0.0, pltpu.roll(center, rows - 1, 0))
        else:
            below = ref[source, y + 1 : y + 1 + rows, :]
        beside = ref[before, y : y + rows, :] + ref[after, y : y + rows, :]
        beside = beside + (above + below)
        beside = beside + jnp.where(lane == 0, 0.0, pltpu.roll(center, 1, 1))
        beside = beside + jnp.where(lane == 511, 0.0, pltpu.roll(center, 511, 1))
        moved = center * keep_rate + beside * spread_rate
        if scale is not None:
            moved = moved * scale
        if y == 0:
            moved = jnp.where(line == 0, 0.0, moved)
        out_ref[target, y : y + rows, :] = moved


def smooth_kernel(edge_ref, mesh_hbm, left_hbm, right_hbm, out_hbm, field, once, arrived, leaving):
    def fetch(k):
        return (
            pltpu.make_async_copy(left_hbm.at[k], field.at[k, pl.ds(0, 2)], arrived.at[k, 0]),
            pltpu.make_async_copy(mesh_hbm.at[k], field.at[k, pl.ds(2, 16)], arrived.at[k, 1]),
            pltpu.make_async_copy(right_hbm.at[k], field.at[k, pl.ds(18, 2)], arrived.at[k, 2]),
        )

    def store(k):
        return pltpu.make_async_copy(field.at[k, pl.ds(2, 16)], out_hbm.at[k], leaving.at[k])

    for k in range(3):
        for copy in fetch(k):
            copy.start()
    for k in range(3):
        for copy in fetch(k):
            copy.wait()
        part = field.at[k]

        def first(x, carry):
            swept(part, once, x + 1, x, True)
            return carry

        def second(x, carry):
            swept(once, part, x + 1, x + 2, False)
            return carry

        swept(part, once, 1, 0, True, edge_ref[0])
        lax.fori_loop(1, 17, first, 0)
        swept(part, once, 18, 17, True, edge_ref[1])
        lax.fori_loop(0, 16, second, 0)
        store(k).start()
    for k in range(3):
        store(k).wait()


def wall_kernel(inter_ref, left_ref, right_ref, tile_ref, out_ref):
    inter = inter_ref[0]
    lane = lax.broadcasted_iota(jnp.int32, (16, 512), 1)
    line = lax.broadcasted_iota(jnp.int32, (16, 512), 0)
    before = jnp.where(line == 0, left_ref[0], pltpu.roll(inter, 1, 0))
    after = jnp.where(line == 15, right_ref[0], pltpu.roll(inter, 15, 0))
    beside = before + after
    beside = beside + jnp.where(lane == 0, 0.0, pltpu.roll(inter, 1, 1))
    beside = beside + jnp.where(lane == 511, 0.0, pltpu.roll(inter, 511, 1))
    first = spread_rate * ((1.0 + keep_rate) * inter + spread_rate * beside)
    second = (spread_rate * spread_rate) * inter
    row = lax.broadcasted_iota(jnp.int32, (8, 512), 0)
    for x in range(16):
        extra = jnp.where(
            row == 0,
            inter[x : x + 1],
            jnp.where(row == 1, first[x : x + 1], jnp.where(row == 2, second[x : x + 1], 0.0)),
        )
        out_ref[0, x] = tile_ref[0, x] + extra


def send_messages(displacement, send_node):
    return pl.pallas_call(
        send_kernel,
        out_shape=jax.ShapeDtypeStruct((24, 8, 128), f32),
        in_specs=[vmem()] * 2,
        out_specs=vmem(),
    )(displacement, send_node.reshape(64, 128))


def cluster_messages(
    table, member_slot, inverse_part, source_coord, target_coord, unity_weight, result_pick
):
    return pl.pallas_call(
        cluster_kernel,
        out_shape=jax.ShapeDtypeStruct((24, 8, 128), f32),
        in_specs=[vmem(), vmem(), pl.BlockSpec(memory_space=pl.ANY)] + [vmem()] * 4,
        out_specs=vmem(),
        scratch_shapes=[
            pltpu.VMEM((4, 1024, 1024), bf16),
            pltpu.SemaphoreType.DMA((4,)),
            pltpu.VMEM((8, 32, 128), f32),
            pltpu.VMEM((8, 128, 128), f32),
            pltpu.VMEM((8, 128, 128), f32),
            pltpu.VMEM((4, 8, 1024), f32),
        ],
        compiler_params=pltpu.CompilerParams(vmem_limit_bytes=40 << 20),
    )(
        table,
        member_slot,
        inverse_part,
        source_coord.transpose(1, 0, 2),
        target_coord.transpose(1, 0, 2),
        unity_weight,
        result_pick.reshape(64, 128),
    )


def scatter(table, receive_vertex):
    return pl.pallas_call(
        scatter_kernel,
        out_shape=jax.ShapeDtypeStruct((3, 16, 512), f32),
        in_specs=[vmem()] * 2,
        out_specs=vmem(),
        scratch_shapes=[
            pltpu.VMEM((576, 512), bf16),
            pltpu.VMEM((128, 512), bf16),
            pltpu.VMEM((576, 128), f32),
        ],
    )(table, receive_vertex.reshape(64, 128))


def smooth(edges, mesh_before, left, right):
    hbm = pl.BlockSpec(memory_space=pl.ANY)
    return pl.pallas_call(
        smooth_kernel,
        out_shape=jax.ShapeDtypeStruct((3, 16, 96, 512), f32),
        in_specs=[pl.BlockSpec(memory_space=pltpu.SMEM), hbm, hbm, hbm],
        out_specs=hbm,
        scratch_shapes=[
            pltpu.VMEM((3, 20, 96, 512), f32),
            pltpu.VMEM((18, 96, 512), f32),
            pltpu.SemaphoreType.DMA((3, 3)),
            pltpu.SemaphoreType.DMA((3,)),
        ],
        compiler_params=pltpu.CompilerParams(vmem_limit_bytes=24 << 20),
    )(edges, mesh_before, left, right)


def add_wall(interface, left, right, field):
    tile = pl.BlockSpec((1, 16, 8, 512), lambda k: (k, 0, 0, 0))
    return pl.pallas_call(
        wall_kernel,
        grid=(3,),
        out_shape=jax.ShapeDtypeStruct((3, 16, 96, 512), f32),
        in_specs=[
            pl.BlockSpec((1, 16, 512), lambda k: (k, 0, 0)),
            pl.BlockSpec((1, 1, 512), lambda k: (k, 0, 0)),
            pl.BlockSpec((1, 1, 512), lambda k: (k, 0, 0)),
            tile,
        ],
        out_specs=tile,
        input_output_aliases={3: 0},
    )(interface, left, right, field)


def local(
    displacement,
    send_node,
    member_slot,
    inverse_part,
    source_coord,
    target_coord,
    unity_weight,
    result_pick,
    receive_vertex,
    mesh_before,
):
    count = lax.axis_size("dev")
    me = lax.axis_index("dev")
    up = [(i, i + 1) for i in range(count - 1)]
    down = [(i + 1, i) for i in range(count - 1)]
    edges = jnp.stack([me > 0, me < count - 1]).astype(f32)

    mesh_left = lax.ppermute(mesh_before[:, 14:16], "dev", up)
    mesh_right = lax.ppermute(mesh_before[:, 0:2], "dev", down)

    messages = send_messages(displacement, send_node)
    table = exchange(messages, 1)
    results = cluster_messages(
        table, member_slot, inverse_part, source_coord, target_coord, unity_weight, result_pick
    )
    returned = exchange(results, 1)
    interface = scatter(returned, receive_vertex)
    wall_left = lax.ppermute(interface[:, 15:16], "dev", up)
    wall_right = lax.ppermute(interface[:, 0:1], "dev", down)
    field = smooth(edges, mesh_before, mesh_left, mesh_right)
    return add_wall(interface, wall_left, wall_right, field)


def solution(mesh):
    in_specs = (
        P(None, "dev"),
        P("dev"),
        P("dev", None),
        P("dev", None, None),
        P("dev", None, None),
        P("dev", None, None),
        P("dev", None),
        P("dev"),
        P("dev"),
        P(None, "dev", None, None),
    )
    out_specs = P(None, "dev", None, None)
    return jax.shard_map(local, mesh=mesh, in_specs=in_specs, out_specs=out_specs, check_vma=False)
```

time: 320 us -> 116 us (0.36)
  the two profiles are of different devices: /device:TPU:32 before, /device:TPU:31 now
where the time goes in v1:
time: 116 us
  Pallas kernels  81.8 us (71%)
  starting transfers between devices  19.6 us (17%)
  local copies, waits for them, and re-layouts  13.9 us (12%)
    pallas_call x2, Pallas kernels, exchange(): pl.pallas_call(exchange_kernel, out_shape=jax.ShapeDtypeStruct((16, 12, 1...  32.7 us
    pallas_call x1, Pallas kernels, smooth(): pl.pallas_call(smooth_kernel, out_shape=jax.ShapeDtypeStruct((3, 16, 96,...  22 us
    pallas_call x1, Pallas kernels, cluster_messages(): pl.pallas_call(cluster_kernel, out_shape=jax.ShapeDtypeStruct((24, 8, 128...  12.8 us
    unnamed x22, local copies, waits for them, and re-layouts  9.79 us
    pallas_call x1, Pallas kernels, scatter(): pl.pallas_call(scatter_kernel, out_shape=jax.ShapeDtypeStruct((3, 16, 512...  7.3 us
    ppermute x1, starting transfers between devices, local(): mesh_left = lax.ppermute(mesh_before[:, 14:16], 'dev', up)  7.2 us
    ppermute x1, starting transfers between devices, local(): wall_left = lax.ppermute(interface[:, 15:16], 'dev', up)  6.9 us
    pallas_call x1, Pallas kernels, send_messages(): pl.pallas_call(send_kernel, out_shape=jax.ShapeDtypeStruct((24, 8, 128),...  3.86 us
  transfers between devices with their start and end apart: 4, of which 0 were waited for; matrix products, arithmetic and copies ran while one was open for 1% of the time, Pallas kernels for 68%

profile of v1, /device:TPU:31, one launch (start us, length us, event | category | flops | bytes accessed | tf_op | source)
XLA Modules:
  0.0 115.5 jit_solution(17785010292488723958)
XLA Ops:
  0.0 0.0 copy-start.6
  0.0 0.0 copy-start.8
  0.0 0.0 copy-start.5
  0.0 0.0 copy-start.4
  0.0 0.0 copy-start.7
  0.0 3.3 %fusion = (f32[3,2,96,512]{3,2,1,0:T(8,128)}, f32[3,2,96,512]{3,2,1,0:T(8,128)}) fusion(f32[3,16,96,512]{3,2,1,0:T(8,128)} %mesh_hbm.1), kind=kLoop, calls=%fused_computation.1 | loop fusion | bytes 4718592 | tf_op jit(solution)/shard_map/slice | solution.py:481
  3.3 2.6 %collective-permute-start.3 = (f32[3,2,96,512]{3,2,1,0:T(8,128)}, f32[3,2,96,512]{3,2,1,0:T(8,128)S(1)}, u32[]{:S(2)}, u32[]{:S(2)}) collective-permute-start(f32[3,2,96,512]{3,2,1,0:T(8,128)} %get-tuple-element.5), channel_id=1, source_target_pairs={{1,0},{2,1},{3,2},{4,3},{5,4},{6,5},{7,6},{8,7},{9,8},{10,9},{11,1... | collective-permute-start | bytes 3538952 | tf_op jit(solution)/shard_map/ppermute | solution.py:481
  5.9 7.2 %collective-permute-start.2 = (f32[3,2,96,512]{3,2,1,0:T(8,128)}, f32[3,2,96,512]{3,2,1,0:T(8,128)S(1)}, u32[]{:S(2)}, u32[]{:S(2)}) collective-permute-start(f32[3,2,96,512]{3,2,1,0:T(8,128)} %get-tuple-element.6), channel_id=1, source_target_pairs={{0,1},{1,2},{2,3},{3,4},{4,5},{5,6},{6,7},{7,8},{8,9},{9,10},{10,1... | collective-permute-start | bytes 3538952 | tf_op jit(solution)/shard_map/ppermute | solution.py:480
  13.1 3.9 %shard_map.100 = f32[24,8,128]{2,1,0:T(8,128)} custom-call(f32[3,4096]{1,0:T(4,128)} %disp_ref.1, s32[64,128]{1,0:T(8,128)} %bitcast.14), custom_call_target="tpu_custom_call" | custom-call | tf_op jit(solution)/shard_map/pallas_call | solution.py:378
  17.0 16.4 %shard_map.101.t_ref = f32[16,12,128]{2,1,0:T(8,128)} custom-call(f32[192,128]{1,0:T(8,128)} %bitcast.13), custom_call_target="tpu_custom_call" | custom-call | tf_op jit(solution)/shard_map/pallas_call | solution.py:128
  33.4 0.0 copy-done.6
  33.4 0.0 copy-done.8
  33.4 0.0 copy-done.5
  33.5 0.0 copy-done.4
  33.5 0.0 copy-done.7
  33.5 0.0 copy-start.1
  33.5 3.4 %copy-done.1 = bf16[4,1024,1024]{2,1,0:T(8,128)(2,1)S(1)} copy-done((bf16[4,1024,1024]{2,1,0:T(8,128)(2,1)S(1)}, bf16[4,1024,1024]{2,1,0:T(8,128)(2,1)}, u32[]{:S(2)}) %copy-start.1) | copy-done | bytes 8388632
  36.9 0.0 copy-start.2
  36.9 0.9 copy-done.2
  37.8 12.8 %shard_map.102 = f32[24,8,128]{2,1,0:T(8,128)S(1)} custom-call(f32[16,12,128]{2,1,0:T(8,128)S(1)} %copy-done.2, s32[4,1024]{1,0:T(4,128)S(1)} %copy-done.7, bf16[4,1024,1024]{2,1,0:T(8,128)(2,1)S(1)} %copy-done.1, f32[3,4,1024]{2,1,0:T(4,128)S(1)} %bitcast.10, f32[3,4,1024]{2,1,0:T(4,128)S(1)} %bitcast.11, f32[4,1024]{1,0:T(4,128)S(1)} %copy-done.8, ...), custom_call_target="tpu_custom_call" | custom-call | tf_op jit(solution)/shard_map/pallas_call | solution.py:389
  50.6 0.0 copy-start.3
  50.6 0.6 copy-done.3
  51.2 16.2 %shard_map.103.t_ref = f32[16,12,128]{2,1,0:T(8,128)} custom-call(f32[192,128]{1,0:T(8,128)} %bitcast.9), custom_call_target="tpu_custom_call" | custom-call | tf_op jit(solution)/shard_map/pallas_call | solution.py:128
  67.5 7.3 %shard_map.104.inter_ref = f32[3,16,512]{2,1,0:T(8,128)} custom-call(f32[16,12,128]{2,1,0:T(8,128)} %shard_map.103.t_ref, s32[64,128]{1,0:T(8,128)} %bitcast.15), custom_call_target="tpu_custom_call" | custom-call | tf_op jit(solution)/shard_map/pallas_call | solution.py:415
  74.8 0.8 fusion.1
  75.6 2.9 %collective-permute-start.1 = (f32[3,1,512]{2,1,0:T(1,128)S(1)}, f32[3,1,512]{2,1,0:T(1,128)S(1)}, u32[]{:S(2)}, u32[]{:S(2)}) collective-permute-start(f32[3,1,512]{2,1,0:T(1,128)S(1)} %get-tuple-element.7), channel_id=1, source_target_pairs={{1,0},{2,1},{3,2},{4,3},{5,4},{6,5},{7,6},{8,7},{9,8},{10,9},{11,1... | collective-permute-start | bytes 18440 | tf_op jit(solution)/shard_map/ppermute | solution.py:491
  78.5 6.9 %collective-permute-start = (f32[3,1,512]{2,1,0:T(1,128)S(1)}, f32[3,1,512]{2,1,0:T(1,128)S(1)}, u32[]{:S(2)}, u32[]{:S(2)}) collective-permute-start(f32[3,1,512]{2,1,0:T(1,128)S(1)} %get-tuple-element.8), channel_id=1, source_target_pairs={{0,1},{1,2},{2,3},{3,4},{4,5},{5,6},{6,7},{7,8},{8,9},{9,10},{10,1... | collective-permute-start | bytes 18440 | tf_op jit(solution)/shard_map/ppermute | solution.py:490
  85.4 0.1 add_convert_fusion.edge_ref
  85.5 0.0 collective-permute-done.3.right_hbm
  85.5 0.0 collective-permute-done.2.left_hbm
  85.5 0.0 copy-start
  85.5 3.7 %copy-done = f32[3,16,96,512]{3,2,1,0:T(8,128)S(1)} copy-done((f32[3,16,96,512]{3,2,1,0:T(8,128)S(1)}, f32[3,16,96,512]{3,2,1,0:T(8,128)}, u32[]{:S(2)}) %copy-start) | copy-done | bytes 9437208
  89.2 22.0 %shard_map.105.tile_ref = f32[3,16,96,512]{3,2,1,0:T(8,128)} custom-call(f32[2]{0:T(128)S(1)} %add_convert_fusion.edge_ref, f32[3,16,96,512]{3,2,1,0:T(8,128)S(1)} %copy-done, f32[3,2,96,512]{3,2,1,0:T(8,128)S(1)} %collective-permute-done.2.left_hbm, f32[3,2,96,512]{3,2,1,0:T(8,128)S(1)} %collective-permute-done.3.right_hbm), custom_call_target="tpu_custom_call" | custom-call | tf_op jit(solution)/shard_map/pallas_call | solution.py:430
  111.2 0.0 collective-permute-done.1.right_ref
  111.2 0.0 copy-start.9
  111.2 0.0 collective-permute-done.left_ref
  111.2 0.6 copy-done.9
  111.8 0.0 copy-start.10
  111.8 0.6 copy-done.10
  112.4 3.1 %shard_map.106 = f32[3,16,96,512]{3,2,1,0:T(8,128)} custom-call(f32[3,16,512]{2,1,0:T(8,128)} %shard_map.104.inter_ref, f32[3,1,512]{2,1,0:T(1,128)} %copy-done.10, f32[3,1,512]{2,1,0:T(1,128)} %copy-done.9, f32[3,16,96,512]{3,2,1,0:T(8,128)} %shard_map.105.tile_ref), custom_call_target="tpu_custom_call", output_to_operand_aliasing={{}: (3, {})} | custom-call | tf_op jit(solution)/shard_map/pallas_call | solution.py:447
Async XLA Ops:
  0.0 33.4 %copy-start.6 = (s32[8192]{0:T(1024)S(1)}, s32[8192]{0:T(1024)}, u32[]{:S(2)}) copy-start(s32[8192]{0:T(1024)} %param.17) | copy-start | bytes 98308
  0.0 33.4 %copy-start.8 = (f32[4,1024]{1,0:T(4,128)S(1)}, f32[4,1024]{1,0:T(4,128)}, u32[]{:S(2)}) copy-start(f32[4,1024]{1,0:T(4,128)} %weight_ref.1) | copy-start | bytes 49156
  0.0 33.4 %copy-start.5 = (f32[4,3,1024]{2,0,1:T(4,128)S(1)}, f32[4,3,1024]{2,0,1:T(4,128)}, u32[]{:S(2)}) copy-start(f32[4,3,1024]{2,0,1:T(4,128)} %param.15) | copy-start | bytes 147460
  0.0 33.4 %copy-start.4 = (f32[4,3,1024]{2,0,1:T(4,128)S(1)}, f32[4,3,1024]{2,0,1:T(4,128)}, u32[]{:S(2)}) copy-start(f32[4,3,1024]{2,0,1:T(4,128)} %param.14) | copy-start | bytes 147460
  0.0 33.4 %copy-start.7 = (s32[4,1024]{1,0:T(4,128)S(1)}, s32[4,1024]{1,0:T(4,128)}, u32[]{:S(2)}) copy-start(s32[4,1024]{1,0:T(4,128)} %slot_ref.1) | copy-start | bytes 49156
  3.3 82.2 %collective-permute-start.3 = (f32[3,2,96,512]{3,2,1,0:T(8,128)}, f32[3,2,96,512]{3,2,1,0:T(8,128)S(1)}, u32[]{:S(2)}, u32[]{:S(2)}) collective-permute-start(f32[3,2,96,512]{3,2,1,0:T(8,128)} %get-tuple-element.5), channel_id=1, source_target_pairs={{1,0},{2,1},{3,2},{4,3},{5,4},{6,5},{7,6},{8,7},{9,8},{10,9},{11,1... | collective-permute-start | bytes 3538952 | tf_op jit(solution)/shard_map/ppermute | solution.py:481
  5.9 79.6 %collective-permute-start.2 = (f32[3,2,96,512]{3,2,1,0:T(8,128)}, f32[3,2,96,512]{3,2,1,0:T(8,128)S(1)}, u32[]{:S(2)}, u32[]{:S(2)}) collective-permute-start(f32[3,2,96,512]{3,2,1,0:T(8,128)} %get-tuple-element.6), channel_id=1, source_target_pairs={{0,1},{1,2},{2,3},{3,4},{4,5},{5,6},{6,7},{7,8},{8,9},{9,10},{10,1... | collective-permute-start | bytes 3538952 | tf_op jit(solution)/shard_map/ppermute | solution.py:480
  33.5 3.4 %copy-start.1 = (bf16[4,1024,1024]{2,1,0:T(8,128)(2,1)S(1)}, bf16[4,1024,1024]{2,1,0:T(8,128)(2,1)}, u32[]{:S(2)}) copy-start(bf16[4,1024,1024]{2,1,0:T(8,128)(2,1)} %inv_hbm.1) | copy-start | bytes 25165828
  36.9 0.9 copy-start.2
  50.6 0.6 copy-start.3
  75.6 35.6 %collective-permute-start.1 = (f32[3,1,512]{2,1,0:T(1,128)S(1)}, f32[3,1,512]{2,1,0:T(1,128)S(1)}, u32[]{:S(2)}, u32[]{:S(2)}) collective-permute-start(f32[3,1,512]{2,1,0:T(1,128)S(1)} %get-tuple-element.7), channel_id=1, source_target_pairs={{1,0},{2,1},{3,2},{4,3},{5,4},{6,5},{7,6},{8,7},{9,8},{10,9},{11,1... | collective-permute-start | bytes 18440 | tf_op jit(solution)/shard_map/ppermute | solution.py:491
  78.5 32.7 %collective-permute-start = (f32[3,1,512]{2,1,0:T(1,128)S(1)}, f32[3,1,512]{2,1,0:T(1,128)S(1)}, u32[]{:S(2)}, u32[]{:S(2)}) collective-permute-start(f32[3,1,512]{2,1,0:T(1,128)S(1)} %get-tuple-element.8), channel_id=1, source_target_pairs={{0,1},{1,2},{2,3},{3,4},{4,5},{5,6},{6,7},{7,8},{8,9},{9,10},{10,1... | collective-permute-start | bytes 18440 | tf_op jit(solution)/shard_map/ppermute | solution.py:490
  85.5 3.7 %copy-start = (f32[3,16,96,512]{3,2,1,0:T(8,128)S(1)}, f32[3,16,96,512]{3,2,1,0:T(8,128)}, u32[]{:S(2)}) copy-start(f32[3,16,96,512]{3,2,1,0:T(8,128)} %mesh_hbm.1) | copy-start | bytes 28311556
  111.2 0.6 copy-start.9
  111.8 0.6 copy-start.10

commit v2 on v1

v2 whole, which is shorter than its diff:
```python
import jax
import jax.numpy as jnp
from jax import lax
from jax.experimental import pallas as pl
from jax.experimental.pallas import tpu as pltpu
from jax.sharding import PartitionSpec as P

relax_rate = 0.8
kernel_sharpness = 8.0
log2_e = 1.4426950408889634
spread_rate = relax_rate / 6.0
keep_rate = 1.0 - relax_rate

MESH = pl.DeviceIdType.MESH
f32 = jnp.float32
bf16 = jnp.bfloat16


def vmem():
    return pl.BlockSpec(memory_space=pltpu.VMEM)


def lookup(row, lanes):
    spread = jnp.broadcast_to(row, lanes.shape)
    return jnp.take_along_axis(spread, lanes, axis=1, mode="promise_in_bounds")


def message_index(index_ref, step):
    x, core = step // 2, step % 2
    even = index_ref[pl.ds(x, 8, stride=8), :]
    odd = index_ref[pl.ds(4 + x, 8, stride=8), :]
    lane = lax.broadcasted_iota(jnp.int32, (8, 128), 1)
    if core == 0:
        return jnp.where(lane < 64, even, pltpu.roll(odd, 64, 1))
    return jnp.where(lane < 64, pltpu.roll(even, 64, 1), odd)


def pick_messages(index_ref, row_of, out_ref):
    for half in range(2):
        index = [message_index(index_ref, 4 * half + g) for g in range(4)]
        high = [jnp.right_shift(i, 7) for i in index]
        low = [jnp.bitwise_and(i, 127) for i in index]
        total = [[jnp.zeros((8, 128), f32) for _ in range(3)] for _ in range(4)]
        for r in range(32):
            hit = [h == r for h in high]
            for k in range(3):
                row = row_of(k, r)
                for g in range(4):
                    total[g][k] = jnp.where(hit[g], lookup(row, low[g]), total[g][k])
        for g in range(4):
            for k in range(3):
                top = ((4 * half + g) * 3 + k) * 8
                out_ref[top : top + 8, :] = total[g][k]


def three_parts(value):
    high = value.astype(bf16).astype(f32)
    rest = value - high
    middle = rest.astype(bf16).astype(f32)
    return high, middle, rest - middle


def cluster_rows(ref, c, rows):
    return jnp.concatenate([ref[q, pl.ds(c, rows, stride=4), :] for q in range(8)], axis=1)


def remote(source, target, send, receive, device):
    copy = pltpu.make_async_remote_copy(
        src_ref=source,
        dst_ref=target,
        send_sem=send,
        recv_sem=receive,
        device_id=(device,),
        device_id_type=MESH,
    )
    copy.start()
    return copy


def first_stage(messages, held, send, receive, outer, inner):
    copies = []
    for i in range(1, 8):
        p = (inner + i) % 8
        copies.append(
            remote(
                messages.at[pl.ds(pl.multiple_of(p * 24, 8), 24)],
                held.at[pl.ds(pl.multiple_of(inner * 24, 8), 24)],
                send.at[i - 1],
                receive.at[i - 1],
                outer * 8 + p,
            )
        )
    mine = pl.ds(pl.multiple_of(inner * 24, 8), 24)
    held[mine, :] = messages[mine, :]
    return copies


def second_stage(held, ready, landed, send, receive, outer, inner):
    lane = lax.broadcasted_iota(jnp.int32, (4, 128), 1)
    for m in range(8):
        for k in range(3):
            first = held[pl.ds(k * 8 + m, 4, stride=48), :]
            second = held[pl.ds(24 + k * 8 + m, 4, stride=48), :]
            ready[2 * m, 4 * k : 4 * k + 4, :] = jnp.where(
                lane < 64, first, pltpu.roll(second, 64, 1)
            )
            ready[2 * m + 1, 4 * k : 4 * k + 4, :] = jnp.where(
                lane < 64, pltpu.roll(first, 64, 1), second
            )
    copies = []
    for i in range(1, 16):
        p = (outer + i) % 16
        copies.append(
            remote(
                ready.at[p],
                landed.at[outer],
                send.at[i - 1],
                receive.at[i - 1],
                p * 8 + inner,
            )
        )
    landed[outer] = ready[outer]
    return copies


def finish(copies):
    for copy in copies:
        copy.wait()


def exponent_rows(source_ref, target_ref, left, right):
    left[...] = jnp.zeros_like(left)
    right[...] = jnp.zeros_like(right)
    ones = jnp.ones((4, 1024), f32)
    source_norm = jnp.zeros((4, 1024), f32)
    target_norm = jnp.zeros((4, 1024), f32)
    pairs = []
    for d in range(3):
        s = source_ref[d]
        t = target_ref[d]
        source_norm += s * s
        target_norm += t * t
        sh, sm, sl = three_parts(s)
        th, tm, tl = three_parts(t * (2.0 * kernel_sharpness * log2_e))
        pairs += [(sh, th), (sh, tm), (sm, th), (sh, tl), (sl, th), (sm, tm)]
    pairs += [(p, ones) for p in three_parts(source_norm * (-kernel_sharpness * log2_e))]
    pairs += [(ones, p) for p in three_parts(target_norm * (-kernel_sharpness * log2_e))]
    for row, (a, b) in enumerate(pairs):
        for q in range(8):
            left[q, 4 * row : 4 * row + 4, :] = a[:, 128 * q : 128 * (q + 1)]
            right[q, 4 * row : 4 * row + 4, :] = b[:, 128 * q : 128 * (q + 1)]


def kernel_values(c, left, right, upper, lower):
    source_rows = cluster_rows(left, c, 32).T.astype(bf16)
    target_rows = cluster_rows(right, c, 32).astype(bf16)
    for p in range(4):
        rows = slice(256 * p, 256 * (p + 1))
        kernel = jnp.exp2(jnp.dot(source_rows[rows], target_rows, preferred_element_type=f32))
        high = kernel.astype(bf16)
        upper[c, rows, :] = high
        lower[c, rows, :] = (kernel - high.astype(f32)).astype(bf16)


def gather_members(table, slot_ref, member):
    member[...] = jnp.zeros_like(member)
    index = [
        jnp.concatenate(
            [slot_ref[:, 256 * m : 256 * m + 128], slot_ref[:, 256 * m + 128 : 256 * m + 256]],
            axis=0,
        )
        for m in range(4)
    ]
    high = [jnp.right_shift(i, 7) for i in index]
    low = [jnp.bitwise_and(i, 127) for i in index]

    def gather(zy, total):
        total = list(total)
        for j in range(4):
            hit = [h == zy * 4 + j for h in high]
            for k in range(3):
                line = table[zy, 4 * k + j : 4 * k + j + 1, :]
                for m in range(4):
                    total[3 * m + k] = jnp.where(hit[m], lookup(line, low[m]), total[3 * m + k])
        return tuple(total)

    total = lax.fori_loop(
        0, 16, gather, tuple(jnp.zeros((8, 128), f32) for _ in range(12))
    )
    for m in range(4):
        for k in range(3):
            value = total[3 * m + k]
            member[2 * m, 4 * k : 4 * k + 4, :] = value[0:4]
            member[2 * m + 1, 4 * k : 4 * k + 4, :] = value[4:8]


def contribute(c, member, inverse, upper, lower, weight_ref, result):
    members = cluster_rows(member, c, 8)
    padded = jnp.concatenate([members, jnp.zeros((8, 1024), f32)], axis=0)
    coupling = lax.dot_general(
        padded.astype(bf16), inverse[c], (((1,), (1,)), ((), ())), preferred_element_type=f32
    )
    coefficient = members + coupling[0:8]
    high = coefficient.astype(bf16).astype(f32)
    both = jnp.concatenate([high, coefficient - high], axis=0).astype(bf16)
    summed = jnp.dot(both, upper[c], preferred_element_type=f32)
    summed += jnp.dot(both, lower[c], preferred_element_type=f32)
    result[c] = (summed[0:8] + summed[8:16]) * weight_ref[c : c + 1, :]


def scatter(table, vertex_ref, values, places, total, out_ref):
    def chunk(zy, carry):
        for j in range(4):
            vertex = vertex_ref[pl.ds(zy * 4 + j, 1), :]
            high = jnp.broadcast_to(jnp.right_shift(vertex, 7), (64, 128))
            low = jnp.broadcast_to(jnp.bitwise_and(vertex, 127), (128, 128))
            at_high = high == lax.broadcasted_iota(jnp.int32, (64, 128), 0)
            at_low = low == lax.broadcasted_iota(jnp.int32, (128, 128), 0)
            lanes = slice(128 * j, 128 * j + 128)
            places[:, lanes] = jnp.where(at_low, 1.0, 0.0).astype(bf16)
            for k in range(3):
                value = table[zy, 4 * k + j : 4 * k + j + 1, :]
                for s, part in enumerate(three_parts(value)):
                    spread = jnp.broadcast_to(part, (64, 128))
                    top = (3 * k + s) * 64
                    values[top : top + 64, lanes] = jnp.where(at_high, spread, 0.0).astype(bf16)
        product = lax.dot_general(
            values[...], places[...], (((1,), (1,)), ((), ())), preferred_element_type=f32
        )
        total[...] += product
        return carry

    total[...] = jnp.zeros_like(total)
    lax.fori_loop(0, 16, chunk, 0)
    for k in range(3):
        top = 3 * k * 64
        for q in range(4):
            out_ref[k, :, 128 * q : 128 * (q + 1)] = (
                total[pl.ds(top + q, 16, stride=4), :]
                + total[pl.ds(top + 64 + q, 16, stride=4), :]
                + total[pl.ds(top + 128 + q, 16, stride=4), :]
            )


def transfer_kernel(
    disp_ref, node_ref, slot_ref, source_ref, target_ref, weight_ref, pick_ref, vertex_ref,
    inv_hbm, mesh_hbm,
    inter_ref, edge_ref, left_hbm, right_hbm,
    messages, held, ready, landed, messages2, held2, ready2, landed2,
    inverse, member, left, right, upper, lower, result, values, places, total, ends, near,
    loaded, send1, recv1, send2, recv2, send3, recv3, send4, recv4, send5, recv5,
):
    me = lax.axis_index("dev")
    outer, inner = me // 8, me % 8
    before, after = (me + 127) % 128, (me + 1) % 128

    barrier = pltpu.get_barrier_semaphore()
    peers = [outer * 8 + (inner + i) % 8 for i in range(1, 8)]
    peers += [((outer + i) % 16) * 8 + inner for i in range(1, 16)]
    peers += [before, after]
    for peer in peers:
        pl.semaphore_signal(barrier, inc=1, device_id=(peer,), device_id_type=MESH)
    loads = [pltpu.make_async_copy(inv_hbm.at[c], inverse.at[c], loaded.at[c]) for c in range(4)]
    for load in loads:
        load.start()

    pick_messages(
        node_ref, lambda k, r: disp_ref[k : k + 1, r * 128 : (r + 1) * 128], messages
    )
    pl.semaphore_wait(barrier, 24)

    copies = first_stage(messages, held, send1, recv1, outer, inner)
    exponent_rows(source_ref, target_ref, left, right)
    kernel_values(0, left, right, upper, lower)
    finish(copies)
    copies = second_stage(held, ready, landed, send2, recv2, outer, inner)
    halos = [
        remote(mesh_hbm.at[:, pl.ds(14, 2)], left_hbm, send5.at[0], recv5.at[0], after),
        remote(mesh_hbm.at[:, pl.ds(0, 2)], right_hbm, send5.at[1], recv5.at[1], before),
    ]
    for c in range(1, 4):
        kernel_values(c, left, right, upper, lower)
    finish(copies)

    gather_members(landed, slot_ref, member)
    for c in range(4):
        loads[c].wait()
        contribute(c, member, inverse, upper, lower, weight_ref, result)
    pick_messages(
        pick_ref,
        lambda k, r: result[r // 8, k : k + 1, (r % 8) * 128 : (r % 8 + 1) * 128],
        messages2,
    )
    finish(first_stage(messages2, held2, send3, recv3, outer, inner))
    finish(second_stage(held2, ready2, landed2, send4, recv4, outer, inner))

    scatter(landed2, vertex_ref, values, places, total, inter_ref)
    ends[...] = jnp.zeros_like(ends)
    for k in range(3):
        ends[0, k : k + 1, :] = inter_ref[k, 0:1, :]
        ends[1, k : k + 1, :] = inter_ref[k, 15:16, :]
    edges = [
        remote(ends.at[1], near.at[0], send5.at[2], recv5.at[2], after),
        remote(ends.at[0], near.at[1], send5.at[3], recv5.at[3], before),
    ]
    finish(edges)
    edge_ref[...] = near[...]
    finish(halos)


def swept(ref, out_ref, source, target, inside=None):
    rows = 16
    lane = lax.broadcasted_iota(jnp.int32, (rows, 512), 1)
    line = lax.broadcasted_iota(jnp.int32, (rows, 512), 0)
    for y in range(0, 96, rows):
        center = ref[source, y : y + rows, :]
        if y == 0:
            above = pltpu.roll(center, 1, 0)
        else:
            above = ref[source, y - 1 : y - 1 + rows, :]
        if y + rows == 96:
            below = jnp.where(line == rows - 1, 0.0, pltpu.roll(center, rows - 1, 0))
        else:
            below = ref[source, y + 1 : y + 1 + rows, :]
        beside = ref[source - 1, y : y + rows, :] + ref[source + 1, y : y + rows, :]
        beside = beside + (above + below)
        beside = beside + jnp.where(lane == 0, 0.0, pltpu.roll(center, 1, 1))
        beside = beside + jnp.where(lane == 511, 0.0, pltpu.roll(center, 511, 1))
        moved = center * keep_rate + beside * spread_rate
        if y == 0:
            moved = jnp.where(line == 0, center, moved)
        if inside is not None:
            moved = jnp.where(inside, moved, 0.0)
        out_ref[target, y : y + rows, :] = moved


def smooth_kernel(
    place_ref, inter_ref, edge_ref, mesh_hbm, left_hbm, right_hbm, out_hbm,
    field, once, arrived, leaving,
):
    place = place_ref[0]
    has_left, has_right = place > 0, place < 127

    def fetch(k):
        return (
            pltpu.make_async_copy(left_hbm.at[k], field.at[k, pl.ds(0, 2)], arrived.at[k, 0]),
            pltpu.make_async_copy(mesh_hbm.at[k], field.at[k, pl.ds(2, 16)], arrived.at[k, 1]),
            pltpu.make_async_copy(right_hbm.at[k], field.at[k, pl.ds(18, 2)], arrived.at[k, 2]),
        )

    def store(k):
        return pltpu.make_async_copy(field.at[k, pl.ds(2, 16)], out_hbm.at[k], leaving.at[k])

    for k in range(3):
        for copy in fetch(k):
            copy.start()
    for k in range(3):
        for copy in fetch(k):
            copy.wait()
        part = field.at[k]
        for x in range(16):
            part[x + 2, 0:1, :] = inter_ref[k, x : x + 1, :]
        part[1, 0:1, :] = edge_ref[0, k : k + 1, :]
        part[18, 0:1, :] = edge_ref[1, k : k + 1, :]

        @pl.when(jnp.logical_not(has_left))
        def _():
            part[1] = jnp.zeros((96, 512), f32)

        @pl.when(jnp.logical_not(has_right))
        def _():
            part[18] = jnp.zeros((96, 512), f32)

        def first(x, carry):
            swept(part, once, x + 1, x)
            return carry

        def second(x, carry):
            swept(once, part, x + 1, x + 2)
            return carry

        swept(part, once, 1, 0, has_left)
        lax.fori_loop(1, 17, first, 0)
        swept(part, once, 18, 17, has_right)
        lax.fori_loop(0, 16, second, 0)
        store(k).start()
    for k in range(3):
        store(k).wait()


def transfer(
    displacement, send_node, member_slot, inverse_part, source_coord, target_coord,
    unity_weight, result_pick, receive_vertex, mesh_before,
):
    hbm = pl.BlockSpec(memory_space=pl.ANY)
    dma = pltpu.SemaphoreType.DMA
    halo = jax.ShapeDtypeStruct((3, 2, 96, 512), f32)
    exchange = [
        pltpu.VMEM((192, 128), f32),
        pltpu.VMEM((192, 128), f32),
        pltpu.VMEM((16, 12, 128), f32),
        pltpu.VMEM((16, 12, 128), f32),
    ]
    return pl.pallas_call(
        transfer_kernel,
        out_shape=(
            jax.ShapeDtypeStruct((3, 16, 512), f32),
            jax.ShapeDtypeStruct((2, 8, 512), f32),
            halo,
            halo,
        ),
        in_specs=[vmem()] * 8 + [hbm, hbm],
        out_specs=(vmem(), vmem(), hbm, hbm),
        scratch_shapes=exchange
        + exchange
        + [
            pltpu.VMEM((4, 1024, 1024), bf16),
            pltpu.VMEM((8, 32, 128), f32),
            pltpu.VMEM((8, 128, 128), f32),
            pltpu.VMEM((8, 128, 128), f32),
            pltpu.VMEM((4, 1024, 1024), bf16),
            pltpu.VMEM((4, 1024, 1024), bf16),
            pltpu.VMEM((4, 8, 1024), f32),
            pltpu.VMEM((576, 512), bf16),
            pltpu.VMEM((128, 512), bf16),
            pltpu.VMEM((576, 128), f32),
            pltpu.VMEM((2, 8, 512), f32),
            pltpu.VMEM((2, 8, 512), f32),
            dma((4,)),
            dma((7,)),
            dma((7,)),
            dma((15,)),
            dma((15,)),
            dma((7,)),
            dma((7,)),
            dma((15,)),
            dma((15,)),
            dma((4,)),
            dma((4,)),
        ],
        compiler_params=pltpu.CompilerParams(
            collective_id=1, has_side_effects=True, vmem_limit_bytes=48 << 20
        ),
    )(
        displacement,
        send_node.reshape(64, 128),
        member_slot,
        source_coord.transpose(1, 0, 2),
        target_coord.transpose(1, 0, 2),
        unity_weight,
        result_pick.reshape(64, 128),
        receive_vertex.reshape(64, 128),
        inverse_part,
        mesh_before,
    )


def smooth(place, interface, edges, mesh_before, left, right):
    hbm = pl.BlockSpec(memory_space=pl.ANY)
    return pl.pallas_call(
        smooth_kernel,
        out_shape=jax.ShapeDtypeStruct((3, 16, 96, 512), f32),
        in_specs=[pl.BlockSpec(memory_space=pltpu.SMEM), vmem(), vmem(), hbm, hbm, hbm],
        out_specs=hbm,
        scratch_shapes=[
            pltpu.VMEM((3, 20, 96, 512), f32),
            pltpu.VMEM((18, 96, 512), f32),
            pltpu.SemaphoreType.DMA((3, 3)),
            pltpu.SemaphoreType.DMA((3,)),
        ],
        compiler_params=pltpu.CompilerParams(vmem_limit_bytes=56 << 20),
    )(place, interface, edges, mesh_before, left, right)


def local(
    displacement,
    send_node,
    member_slot,
    inverse_part,
    source_coord,
    target_coord,
    unity_weight,
    result_pick,
    receive_vertex,
    mesh_before,
):
    place = lax.axis_index("dev").astype(jnp.int32).reshape(1)
    interface, edges, left, right = transfer(
        displacement, send_node, member_slot, inverse_part, source_coord, target_coord,
        unity_weight, result_pick, receive_vertex, mesh_before,
    )
    return smooth(place, interface, edges, mesh_before, left, right)


def solution(mesh):
    in_specs = (
        P(None, "dev"),
        P("dev"),
        P("dev", None),
        P("dev", None, None),
        P("dev", None, None),
        P("dev", None, None),
        P("dev", None),
        P("dev"),
        P("dev"),
        P(None, "dev", None, None),
    )
    out_specs = P(None, "dev", None, None)
    return jax.shard_map(local, mesh=mesh, in_specs=in_specs, out_specs=out_specs, check_vma=False)
```

time: 116 us -> 89.6 us (0.77)
  the two profiles are of different devices: /device:TPU:31 before, /device:TPU:0 now
where the time goes in v2:
time: 89.6 us; the launch traced here: 89 us
  Pallas kernels  79.5 us (89%)
  local copies, waits for them, and re-layouts  9.42 us (11%)
    pallas_call x1, Pallas kernels, transfer(): pl.pallas_call(transfer_kernel, out_shape=(jax.ShapeDtypeStruct((3, 16, 5...  57 us
    pallas_call x1, Pallas kernels, smooth(): pl.pallas_call(smooth_kernel, out_shape=jax.ShapeDtypeStruct((3, 16, 96,...  22.6 us
    unnamed x24, local copies, waits for them, and re-layouts  9.42 us

profile of v2, /device:TPU:0, one launch (start us, length us, event | category | flops | bytes accessed | tf_op | source)
XLA Modules:
  0.0 89.0 jit_solution(12872985963862613052)
XLA Ops:
  0.0 0.0 copy-start.3
  0.0 0.8 copy-done.3
  0.8 0.0 copy-start.4
  0.8 0.8 copy-done.4
  1.6 0.0 copy-start.5
  1.6 0.8 copy-done.5
  2.4 0.0 copy-start.6
  2.4 0.8 copy-done.6
  3.2 0.0 copy-start.7
  3.2 0.8 copy-done.7
  4.0 0.0 copy-start.8
  4.0 0.8 copy-done.8
  4.7 0.0 copy-start.10
  4.7 0.7 copy-done.10
  5.4 0.0 copy-start.11
  5.4 0.7 copy-done.11
  6.1 57.0 %shard_map.100 = (f32[3,16,512]{2,1,0:T(8,128)S(1)}, f32[2,8,512]{2,1,0:T(8,128)S(1)}, f32[3,2,96,512]{3,2,1,0:T(8,128)S(1)}, f32[3,2,96,512]{3,2,1,0:T(8,128)S(1)}) custom-call(f32[3,4096]{1,0:T(4,128)S(1)} %copy-done.3, s32[64,128]{1,0:T(8,128)S(1)} %bitcast.8, s32[4,1024]{1,0:T(4,128)S(1)} %copy-done.10, f32[3,4,1024]{2,1,0:T(4,128)S(1)} %bitcast.6, ...), custom_call_target="tpu_custom_call" | custom-call | tf_op jit(solution)/shard_map/pallas_call | solution.py:404
  63.1 0.0 copy-start
  63.1 1.0 %copy-done = f32[3,2,96,512]{3,2,1,0:T(8,128)} copy-done((f32[3,2,96,512]{3,2,1,0:T(8,128)}, f32[3,2,96,512]{3,2,1,0:T(8,128)S(1)}, u32[]{:S(2)}) %copy-start) | copy-done | bytes 1179672
  64.2 0.0 copy-start.1
  64.2 1.0 %copy-done.1 = f32[3,2,96,512]{3,2,1,0:T(8,128)} copy-done((f32[3,2,96,512]{3,2,1,0:T(8,128)}, f32[3,2,96,512]{3,2,1,0:T(8,128)S(1)}, u32[]{:S(2)}) %copy-start.1) | copy-done | bytes 1179672
  65.2 0.0 copy-start.2
  65.2 0.6 copy-done.2
  65.8 0.0 copy-start.9
  65.8 0.6 copy-done.9
  66.4 22.6 %shard_map.101 = f32[3,16,96,512]{3,2,1,0:T(8,128)} custom-call(s32[1]{0:T(128)} %bitcast.place_ref, f32[3,16,512]{2,1,0:T(8,128)} %copy-done.2, f32[2,8,512]{2,1,0:T(8,128)} %copy-done.9, f32[3,16,96,512]{3,2,1,0:T(8,128)} %mesh_hbm.3, f32[3,2,96,512]{3,2,1,0:T(8,128)} %copy-done, f32[3,2,96,512]{3,2,1,0:T(8,128)} %copy-done.1), custom_call_target="tpu_custom_call" | custom-call | tf_op jit(solution)/shard_map/pallas_call | solution.py:460
Async XLA Ops:
  0.0 0.8 copy-start.3
  0.8 0.8 copy-start.4
  1.6 0.8 copy-start.5
  2.4 0.8 copy-start.6
  3.2 0.8 copy-start.7
  4.0 0.8 copy-start.8
  4.7 0.7 copy-start.10
  5.4 0.7 copy-start.11
  63.1 1.0 %copy-start = (f32[3,2,96,512]{3,2,1,0:T(8,128)}, f32[3,2,96,512]{3,2,1,0:T(8,128)S(1)}, u32[]{:S(2)}) copy-start(f32[3,2,96,512]{3,2,1,0:T(8,128)S(1)} %get-tuple-element.11.left_hbm) | copy-start | bytes 3538948
  64.2 1.0 %copy-start.1 = (f32[3,2,96,512]{3,2,1,0:T(8,128)}, f32[3,2,96,512]{3,2,1,0:T(8,128)S(1)}, u32[]{:S(2)}) copy-start(f32[3,2,96,512]{3,2,1,0:T(8,128)S(1)} %get-tuple-element.12.right_hbm) | copy-start | bytes 3538948
  65.2 0.6 copy-start.2
  65.8 0.6 copy-start.9

commit v3 on v2

--- a/solution.py
+++ b/solution.py
@@ -174,10 +174,11 @@
     high = [jnp.right_shift(i, 7) for i in index]
     low = [jnp.bitwise_and(i, 127) for i in index]
 
-    def gather(zy, total):
+    def gather(part, total):
         total = list(total)
-        for j in range(4):
-            hit = [h == zy * 4 + j for h in high]
+        for r in range(16):
+            zy, j = part * 4 + r // 4, r % 4
+            hit = [h == part * 16 + r for h in high]
             for k in range(3):
                 line = table[zy, 4 * k + j : 4 * k + j + 1, :]
                 for m in range(4):
@@ -185,7 +186,7 @@
         return tuple(total)
 
     total = lax.fori_loop(
-        0, 16, gather, tuple(jnp.zeros((8, 128), f32) for _ in range(12))
+        0, 4, gather, tuple(jnp.zeros((8, 128), f32) for _ in range(12))
     )
     for m in range(4):
         for k in range(3):
@@ -209,103 +210,45 @@
 
 
 def scatter(table, vertex_ref, values, places, total, out_ref):
-    def chunk(zy, carry):
-        for j in range(4):
-            vertex = vertex_ref[pl.ds(zy * 4 + j, 1), :]
-            high = jnp.broadcast_to(jnp.right_shift(vertex, 7), (64, 128))
-            low = jnp.broadcast_to(jnp.bitwise_and(vertex, 127), (128, 128))
-            at_high = high == lax.broadcasted_iota(jnp.int32, (64, 128), 0)
-            at_low = low == lax.broadcasted_iota(jnp.int32, (128, 128), 0)
-            lanes = slice(128 * j, 128 * j + 128)
-            places[:, lanes] = jnp.where(at_low, 1.0, 0.0).astype(bf16)
-            for k in range(3):
-                value = table[zy, 4 * k + j : 4 * k + j + 1, :]
-                for s, part in enumerate(three_parts(value)):
-                    spread = jnp.broadcast_to(part, (64, 128))
-                    top = (3 * k + s) * 64
-                    values[top : top + 64, lanes] = jnp.where(at_high, spread, 0.0).astype(bf16)
-        product = lax.dot_general(
-            values[...], places[...], (((1,), (1,)), ((), ())), preferred_element_type=f32
-        )
+    def chunk(group, carry):
+        product = jnp.zeros((384, 128), f32)
+        for part in range(4):
+            zy = group * 4 + part
+            for j in range(4):
+                vertex = vertex_ref[pl.ds(zy * 4 + j, 1), :]
+                high = jnp.broadcast_to(jnp.right_shift(vertex, 7), (64, 128))
+                low = jnp.broadcast_to(jnp.bitwise_and(vertex, 127), (128, 128))
+                at_high = high == lax.broadcasted_iota(jnp.int32, (64, 128), 0)
+                at_low = low == lax.broadcasted_iota(jnp.int32, (128, 128), 0)
+                lanes = slice(128 * j, 128 * j + 128)
+                places[part, :, lanes] = jnp.where(at_low, 1.0, 0.0).astype(bf16)
+                for k in range(3):
+                    value = table[zy, 4 * k + j : 4 * k + j + 1, :]
+                    upper = value.astype(bf16).astype(f32)
+                    for s, half in enumerate((upper, value - upper)):
+                        spread = jnp.broadcast_to(half, (64, 128))
+                        top = (2 * k + s) * 64
+                        values[part, top : top + 64, lanes] = jnp.where(
+                            at_high, spread, 0.0
+                        ).astype(bf16)
+            product += lax.dot_general(
+                values[part],
+                places[part],
+                (((1,), (1,)), ((), ())),
+                preferred_element_type=f32,
+            )
         total[...] += product
         return carry
 
     total[...] = jnp.zeros_like(total)
-    lax.fori_loop(0, 16, chunk, 0)
+    lax.fori_loop(0, 4, chunk, 0)
     for k in range(3):
-        top = 3 * k * 64
+        top = 2 * k * 64
         for q in range(4):
             out_ref[k, :, 128 * q : 128 * (q + 1)] = (
                 total[pl.ds(top + q, 16, stride=4), :]
                 + total[pl.ds(top + 64 + q, 16, stride=4), :]
-                + total[pl.ds(top + 128 + q, 16, stride=4), :]
             )
-
-
-def transfer_kernel(
-    disp_ref, node_ref, slot_ref, source_ref, target_ref, weight_ref, pick_ref, vertex_ref,
-    inv_hbm, mesh_hbm,
-    inter_ref, edge_ref, left_hbm, right_hbm,
-    messages, held, ready, landed, messages2, held2, ready2, landed2,
-    inverse, member, left, right, upper, lower, result, values, places, total, ends, near,
-    loaded, send1, recv1, send2, recv2, send3, recv3, send4, recv4, send5, recv5,
-):
-    me = lax.axis_index("dev")
-    outer, inner = me // 8, me % 8
-    before, after = (me + 127) % 128, (me + 1) % 128
-
-    barrier = pltpu.get_barrier_semaphore()
-    peers = [outer * 8 + (inner + i) % 8 for i in range(1, 8)]
-    peers += [((outer + i) % 16) * 8 + inner for i in range(1, 16)]
-    peers += [before, after]
-    for peer in peers:
-        pl.semaphore_signal(barrier, inc=1, device_id=(peer,), device_id_type=MESH)
-    loads = [pltpu.make_async_copy(inv_hbm.at[c], inverse.at[c], loaded.at[c]) for c in range(4)]
-    for load in loads:
-        load.start()
-
-    pick_messages(
-        node_ref, lambda k, r: disp_ref[k : k + 1, r * 128 : (r + 1) * 128], messages
-    )
-    pl.semaphore_wait(barrier, 24)
-
-    copies = first_stage(messages, held, send1, recv1, outer, inner)
-    exponent_rows(source_ref, target_ref, left, right)
-    kernel_values(0, left, right, upper, lower)
-    finish(copies)
-    copies = second_stage(held, ready, landed, send2, recv2, outer, inner)
-    halos = [
-        remote(mesh_hbm.at[:, pl.ds(14, 2)], left_hbm, send5.at[0], recv5.at[0], after),
-        remote(mesh_hbm.at[:, pl.ds(0, 2)], right_hbm, send5.at[1], recv5.at[1], before),
-    ]
-    for c in range(1, 4):
-        kernel_values(c, left, right, upper, lower)
-    finish(copies)
-
-    gather_members(landed, slot_ref, member)
-    for c in range(4):
-        loads[c].wait()
-        contribute(c, member, inverse, upper, lower, weight_ref, result)
-    pick_messages(
-        pick_ref,
-        lambda k, r: result[r // 8, k : k + 1, (r % 8) * 128 : (r % 8 + 1) * 128],
-        messages2,
-    )
-    finish(first_stage(messages2, held2, send3, recv3, outer, inner))
-    finish(second_stage(held2, ready2, landed2, send4, recv4, outer, inner))
-
-    scatter(landed2, vertex_ref, values, places, total, inter_ref)
-    ends[...] = jnp.zeros_like(ends)
-    for k in range(3):
-        ends[0, k : k + 1, :] = inter_ref[k, 0:1, :]
-        ends[1, k : k + 1, :] = inter_ref[k, 15:16, :]
-    edges = [
-        remote(ends.at[1], near.at[0], send5.at[2], recv5.at[2], after),
-        remote(ends.at[0], near.at[1], send5.at[3], recv5.at[3], before),
-    ]
-    finish(edges)
-    edge_ref[...] = near[...]
-    finish(halos)
 
 
 def swept(ref, out_ref, source, target, inside=None):
@@ -334,8 +277,175 @@
         out_ref[target, y : y + rows, :] = moved
 
 
+def sweep_once(field, once, has_left, has_right):
+    def plane(x, carry):
+        swept(field, once, x + 1, x)
+        return carry
+
+    swept(field, once, 1, 0, has_left)
+    lax.fori_loop(1, 17, plane, 0)
+    swept(field, once, 18, 17, has_right)
+
+
+def sweep_again(field, once):
+    def plane(x, carry):
+        swept(once, field, x + 1, x + 2)
+        return carry
+
+    lax.fori_loop(0, 16, plane, 0)
+
+
+def close_ends(field, has_left, has_right):
+    @pl.when(jnp.logical_not(has_left))
+    def _():
+        field[1] = jnp.zeros((96, 512), f32)
+
+    @pl.when(jnp.logical_not(has_right))
+    def _():
+        field[18] = jnp.zeros((96, 512), f32)
+
+
+def add_wall(inter, before, after, field):
+    lane = lax.broadcasted_iota(jnp.int32, (16, 512), 1)
+    line = lax.broadcasted_iota(jnp.int32, (16, 512), 0)
+    beside = jnp.where(line == 0, before, pltpu.roll(inter, 1, 0))
+    beside = beside + jnp.where(line == 15, after, pltpu.roll(inter, 15, 0))
+    beside = beside + jnp.where(lane == 0, 0.0, pltpu.roll(inter, 1, 1))
+    beside = beside + jnp.where(lane == 511, 0.0, pltpu.roll(inter, 511, 1))
+    first = spread_rate * ((1.0 + keep_rate) * inter + spread_rate * beside)
+    second = (spread_rate * spread_rate) * inter
+    row = lax.broadcasted_iota(jnp.int32, (8, 512), 0)
+    for x in range(16):
+        extra = jnp.where(
+            row == 0,
+            inter[x : x + 1],
+            jnp.where(row == 1, first[x : x + 1], jnp.where(row == 2, second[x : x + 1], 0.0)),
+        )
+        field[x + 2, 0:8, :] += extra
+
+
+def transfer_kernel(
+    disp_hbm, node_hbm, slot_hbm, source_hbm, target_hbm, weight_hbm, pick_hbm, vertex_hbm,
+    inv_hbm, mesh_hbm,
+    inter_hbm, edge_hbm, left_hbm, right_hbm, part_hbm,
+    disp_ref, node_ref, slot_ref, source_ref, target_ref, weight_ref, pick_ref, vertex_ref,
+    messages, held, ready, landed, messages2, held2, ready2, landed2,
+    inverse, member, left, right, upper, lower, result, values, places, total,
+    inter_ref, ends, near, field, once,
+    fetched, loaded, send1, recv1, send2, recv2, send3, recv3, send4, recv4, send5, recv5, stored,
+):
+    me = lax.axis_index("dev")
+    outer, inner = me // 8, me % 8
+    before, after = (me + 127) % 128, (me + 1) % 128
+    has_left, has_right = me > 0, me < 127
+
+    small = [
+        (disp_hbm, disp_ref), (node_hbm, node_ref), (slot_hbm, slot_ref),
+        (source_hbm, source_ref), (target_hbm, target_ref), (weight_hbm, weight_ref),
+        (pick_hbm, pick_ref), (vertex_hbm, vertex_ref),
+    ]
+    fetches = [pltpu.make_async_copy(a, b, fetched.at[i]) for i, (a, b) in enumerate(small)]
+    for fetch in fetches:
+        fetch.start()
+    barrier = pltpu.get_barrier_semaphore()
+    peers = [outer * 8 + (inner + i) % 8 for i in range(1, 8)]
+    peers += [((outer + i) % 16) * 8 + inner for i in range(1, 16)]
+    peers += [before, after]
+    for peer in peers:
+        pl.semaphore_signal(barrier, inc=1, device_id=(peer,), device_id_type=MESH)
+    loads = [pltpu.make_async_copy(inv_hbm.at[c], inverse.at[c], loaded.at[c]) for c in range(4)]
+    loads.append(pltpu.make_async_copy(mesh_hbm.at[0], field.at[pl.ds(2, 16)], loaded.at[4]))
+    for load in loads:
+        load.start()
+
+    finish(fetches[:2])
+    pick_messages(
+        node_ref, lambda k, r: disp_ref[k : k + 1, r * 128 : (r + 1) * 128], messages
+    )
+    pl.semaphore_wait(barrier, 24)
+
+    copies = first_stage(messages, held, send1, recv1, outer, inner)
+    finish(fetches[2:])
+    exponent_rows(source_ref, target_ref, left, right)
+    kernel_values(0, left, right, upper, lower)
+    kernel_values(1, left, right, upper, lower)
+    finish(copies)
+    copies = second_stage(held, ready, landed, send2, recv2, outer, inner)
+    kernel_values(2, left, right, upper, lower)
+    kernel_values(3, left, right, upper, lower)
+    finish(copies)
+    halos = [
+        remote(
+            mesh_hbm.at[0, pl.ds(14, 2)], field.at[pl.ds(0, 2)], send5.at[0], recv5.at[0], after
+        ),
+        remote(
+            mesh_hbm.at[0, pl.ds(0, 2)], field.at[pl.ds(18, 2)], send5.at[1], recv5.at[1], before
+        ),
+    ]
+
+    gather_members(landed, slot_ref, member)
+    for c in range(4):
+        loads[c].wait()
+        contribute(c, member, inverse, upper, lower, weight_ref, result)
+    pick_messages(
+        pick_ref,
+        lambda k, r: result[r // 8, k : k + 1, (r % 8) * 128 : (r % 8 + 1) * 128],
+        messages2,
+    )
+    loads[4].wait()
+    copies = first_stage(messages2, held2, send3, recv3, outer, inner)
+    finish(halos)
+    field[1, 0:1, :] = jnp.zeros((1, 512), f32)
+    field[18, 0:1, :] = jnp.zeros((1, 512), f32)
+    for x in range(16):
+        field[x + 2, 0:1, :] = jnp.zeros((1, 512), f32)
+    close_ends(field, has_left, has_right)
+    sweep_once(field, once, has_left, has_right)
+    finish(copies)
+    copies = second_stage(held2, ready2, landed2, send4, recv4, outer, inner)
+    sweep_again(field, once)
+    whole = pltpu.make_async_copy(field.at[pl.ds(2, 16)], part_hbm, stored.at[0])
+    whole.start()
+    finish(copies)
+    two = pl.ds(1, 2)
+    halos = [
+        remote(mesh_hbm.at[two, pl.ds(14, 2)], left_hbm, send5.at[2], recv5.at[2], after),
+        remote(mesh_hbm.at[two, pl.ds(0, 2)], right_hbm, send5.at[3], recv5.at[3], before),
+    ]
+
+    scatter(landed2, vertex_ref, values, places, total, inter_ref)
+    ends[...] = jnp.zeros_like(ends)
+    for k in range(3):
+        ends[0, k : k + 1, :] = inter_ref[k, 0:1, :]
+        ends[1, k : k + 1, :] = inter_ref[k, 15:16, :]
+    edges = [
+        remote(ends.at[1], near.at[0], send5.at[4], recv5.at[4], after),
+        remote(ends.at[0], near.at[1], send5.at[5], recv5.at[5], before),
+    ]
+    wall = pltpu.make_async_copy(inter_ref, inter_hbm, stored.at[1])
+    wall.start()
+    whole.wait()
+    finish(edges)
+    edge = pltpu.make_async_copy(near, edge_hbm, stored.at[2])
+    edge.start()
+    add_wall(
+        inter_ref[0],
+        jnp.where(has_left, near[0, 0:1, :], 0.0),
+        jnp.where(has_right, near[1, 0:1, :], 0.0),
+        field,
+    )
+    rows = pltpu.make_async_copy(
+        field.at[pl.ds(2, 16), pl.ds(0, 8)], part_hbm.at[:, pl.ds(0, 8)], stored.at[3]
+    )
+    rows.start()
+    wall.wait()
+    edge.wait()
+    rows.wait()
+    finish(halos)
+
+
 def smooth_kernel(
-    place_ref, inter_ref, edge_ref, mesh_hbm, left_hbm, right_hbm, out_hbm,
+    place_ref, inter_ref, edge_ref, part_hbm, mesh_hbm, left_hbm, right_hbm, out_hbm,
     field, once, arrived, leaving,
 ):
     place = place_ref[0]
@@ -343,48 +453,34 @@
 
     def fetch(k):
         return (
-            pltpu.make_async_copy(left_hbm.at[k], field.at[k, pl.ds(0, 2)], arrived.at[k, 0]),
-            pltpu.make_async_copy(mesh_hbm.at[k], field.at[k, pl.ds(2, 16)], arrived.at[k, 1]),
-            pltpu.make_async_copy(right_hbm.at[k], field.at[k, pl.ds(18, 2)], arrived.at[k, 2]),
+            pltpu.make_async_copy(left_hbm.at[k - 1], field.at[k - 1, pl.ds(0, 2)], arrived.at[k, 0]),
+            pltpu.make_async_copy(mesh_hbm.at[k], field.at[k - 1, pl.ds(2, 16)], arrived.at[k, 1]),
+            pltpu.make_async_copy(
+                right_hbm.at[k - 1], field.at[k - 1, pl.ds(18, 2)], arrived.at[k, 2]
+            ),
         )
 
     def store(k):
-        return pltpu.make_async_copy(field.at[k, pl.ds(2, 16)], out_hbm.at[k], leaving.at[k])
-
-    for k in range(3):
+        return pltpu.make_async_copy(field.at[k - 1, pl.ds(2, 16)], out_hbm.at[k], leaving.at[k])
+
+    for k in (1, 2):
         for copy in fetch(k):
             copy.start()
-    for k in range(3):
-        for copy in fetch(k):
-            copy.wait()
-        part = field.at[k]
+    done = pltpu.make_async_copy(part_hbm, out_hbm.at[0], leaving.at[0])
+    done.start()
+    for k in (1, 2):
+        finish(fetch(k))
+        part = field.at[k - 1]
         for x in range(16):
             part[x + 2, 0:1, :] = inter_ref[k, x : x + 1, :]
         part[1, 0:1, :] = edge_ref[0, k : k + 1, :]
         part[18, 0:1, :] = edge_ref[1, k : k + 1, :]
-
-        @pl.when(jnp.logical_not(has_left))
-        def _():
-            part[1] = jnp.zeros((96, 512), f32)
-
-        @pl.when(jnp.logical_not(has_right))
-        def _():
-            part[18] = jnp.zeros((96, 512), f32)
-
-        def first(x, carry):
-            swept(part, once, x + 1, x)
-            return carry
-
-        def second(x, carry):
-            swept(once, part, x + 1, x + 2)
-            return carry
-
-        swept(part, once, 1, 0, has_left)
-        lax.fori_loop(1, 17, first, 0)
-        swept(part, once, 18, 17, has_right)
-        lax.fori_loop(0, 16, second, 0)
+        close_ends(part, has_left, has_right)
+        sweep_once(part, once, has_left, has_right)
+        sweep_again(part, once)
         store(k).start()
-    for k in range(3):
+    done.wait()
+    for k in (1, 2):
         store(k).wait()
 
 
@@ -394,12 +490,22 @@
 ):
     hbm = pl.BlockSpec(memory_space=pl.ANY)
     dma = pltpu.SemaphoreType.DMA
-    halo = jax.ShapeDtypeStruct((3, 2, 96, 512), f32)
+    halo = jax.ShapeDtypeStruct((2, 2, 96, 512), f32)
     exchange = [
         pltpu.VMEM((192, 128), f32),
         pltpu.VMEM((192, 128), f32),
         pltpu.VMEM((16, 12, 128), f32),
         pltpu.VMEM((16, 12, 128), f32),
+    ]
+    small = [
+        displacement,
+        send_node.reshape(64, 128),
+        member_slot,
+        source_coord.transpose(1, 0, 2),
+        target_coord.transpose(1, 0, 2),
+        unity_weight,
+        result_pick.reshape(64, 128),
+        receive_vertex.reshape(64, 128),
     ]
     return pl.pallas_call(
         transfer_kernel,
@@ -408,10 +514,12 @@
             jax.ShapeDtypeStruct((2, 8, 512), f32),
             halo,
             halo,
+            jax.ShapeDtypeStruct((16, 96, 512), f32),
         ),
-        in_specs=[vmem()] * 8 + [hbm, hbm],
-        out_specs=(vmem(), vmem(), hbm, hbm),
-        scratch_shapes=exchange
+        in_specs=[hbm] * 10,
+        out_specs=(hbm,) * 5,
+        scratch_shapes=[pltpu.VMEM(a.shape, a.dtype) for a in small]
+        + exchange
         + exchange
         + [
             pltpu.VMEM((4, 1024, 1024), bf16),
@@ -421,12 +529,16 @@
             pltpu.VMEM((4, 1024, 1024), bf16),
             pltpu.VMEM((4, 1024, 1024), bf16),
             pltpu.VMEM((4, 8, 1024), f32),
-            pltpu.VMEM((576, 512), bf16),
-            pltpu.VMEM((128, 512), bf16),
-            pltpu.VMEM((576, 128), f32),
+            pltpu.VMEM((4, 384, 512), bf16),
+            pltpu.VMEM((4, 128, 512), bf16),
+            pltpu.VMEM((384, 128), f32),
+            pltpu.VMEM((3, 16, 512), f32),
             pltpu.VMEM((2, 8, 512), f32),
             pltpu.VMEM((2, 8, 512), f32),
-            dma((4,)),
+            pltpu.VMEM((20, 96, 512), f32),
+            pltpu.VMEM((18, 96, 512), f32),
+            dma((8,)),
+            dma((5,)),
             dma((7,)),
             dma((7,)),
             dma((15,)),
@@ -435,41 +547,31 @@
             dma((7,)),
             dma((15,)),
             dma((15,)),
-            dma((4,)),
+            dma((6,)),
+            dma((6,)),
             dma((4,)),
         ],
         compiler_params=pltpu.CompilerParams(
-            collective_id=1, has_side_effects=True, vmem_limit_bytes=48 << 20
+            collective_id=1, has_side_effects=True, vmem_limit_bytes=63 << 20
         ),
-    )(
-        displacement,
-        send_node.reshape(64, 128),
-        member_slot,
-        source_coord.transpose(1, 0, 2),
-        target_coord.transpose(1, 0, 2),
-        unity_weight,
-        result_pick.reshape(64, 128),
-        receive_vertex.reshape(64, 128),
-        inverse_part,
-        mesh_before,
-    )
-
-
-def smooth(place, interface, edges, mesh_before, left, right):
+    )(*small, inverse_part, mesh_before)
+
+
+def smooth(place, interface, edges, part, mesh_before, left, right):
     hbm = pl.BlockSpec(memory_space=pl.ANY)
     return pl.pallas_call(
         smooth_kernel,
         out_shape=jax.ShapeDtypeStruct((3, 16, 96, 512), f32),
-        in_specs=[pl.BlockSpec(memory_space=pltpu.SMEM), vmem(), vmem(), hbm, hbm, hbm],
+        in_specs=[pl.BlockSpec(memory_space=pltpu.SMEM), vmem(), vmem(), hbm, hbm, hbm, hbm],
         out_specs=hbm,
         scratch_shapes=[
-            pltpu.VMEM((3, 20, 96, 512), f32),
+            pltpu.VMEM((2, 20, 96, 512), f32),
             pltpu.VMEM((18, 96, 512), f32),
             pltpu.SemaphoreType.DMA((3, 3)),
             pltpu.SemaphoreType.DMA((3,)),
         ],
-        compiler_params=pltpu.CompilerParams(vmem_limit_bytes=56 << 20),
-    )(place, interface, edges, mesh_before, left, right)
+        compiler_params=pltpu.CompilerParams(vmem_limit_bytes=63 << 20),
+    )(place, interface, edges, part, mesh_before, left, right)
 
 
 def local(
@@ -485,11 +587,11 @@
     mesh_before,
 ):
     place = lax.axis_index("dev").astype(jnp.int32).reshape(1)
-    interface, edges, left, right = transfer(
+    interface, edges, left, right, part = transfer(
         displacement, send_node, member_slot, inverse_part, source_coord, target_coord,
         unity_weight, result_pick, receive_vertex, mesh_before,
     )
-    return smooth(place, interface, edges, mesh_before, left, right)
+    return smooth(place, interface, edges, part, mesh_before, left, right)
 
 
 def solution(mesh):

time: 89.6 us -> 146 us (1.63)
  Pallas kernels: 79.5 us -> 146 us
  local copies, waits for them, and re-layouts: 9.42 us -> 0 us
    pallas_call x1, Pallas kernels: 22.6 us -> 97.4 us  [smooth(): pl.pallas_call(smooth_kernel, out_shape=jax.ShapeDtypeStruct((3, 16, 96,...]
    unnamed x24 -> x0, local copies, waits for them, and re-layouts: 9.42 us -> none
    pallas_call x1, Pallas kernels: 57 us -> 48.3 us  [transfer(): pl.pallas_call(transfer_kernel, out_shape=(jax.ShapeDtypeStruct((3, 16, 5...]
where the time goes in v3:
time: 146 us
  Pallas kernels  146 us (100%)
    pallas_call x1, Pallas kernels, smooth(): pl.pallas_call(smooth_kernel, out_shape=jax.ShapeDtypeStruct((3, 16, 96,...  97.4 us
    pallas_call x1, Pallas kernels, transfer(): pl.pallas_call(transfer_kernel, out_shape=(jax.ShapeDtypeStruct((3, 16, 5...  48.3 us

profile of v3, /device:TPU:0, one launch (start us, length us, event | category | flops | bytes accessed | tf_op | source)
XLA Modules:
  0.0 145.7 jit_solution(9270917548106702197)
XLA Ops:
  0.0 48.3 %shard_map.100 = (f32[3,16,512]{2,1,0:T(8,128)}, f32[2,8,512]{2,1,0:T(8,128)}, f32[2,2,96,512]{3,2,1,0:T(8,128)}, f32[2,2,96,512]{3,2,1,0:T(8,128)}, f32[16,96,512]{2,1,0:T(8,128)}) custom-call(f32[3,4096]{1,0:T(4,128)} %disp_hbm.1, s32[64,128]{1,0:T(8,128)} %bitcast.8, s32[4,1024]{1,0:T(4,128)} %slot_hbm.1, f32[3,4,1024]{2,1,0:T(4,128)} %bitcast.6, ...), custom_call_target="tpu_custom_call" | custom-call | tf_op jit(solution)/shard_map/pallas_call | solution.py:510
  48.3 97.4 %shard_map.101 = f32[3,16,96,512]{3,2,1,0:T(8,128)} custom-call(s32[1]{0:T(128)} %bitcast.place_ref, f32[3,16,512]{2,1,0:T(8,128)} %get-tuple-element.10.inter_ref, f32[2,8,512]{2,1,0:T(8,128)} %get-tuple-element.11.edge_ref, f32[16,96,512]{2,1,0:T(8,128)} %get-tuple-element.12.part_hbm, f32[3,16,96,512]{3,2,1,0:T(8,128)} %mesh_hbm.3, ...), custom_call_target="tpu_custom_call" | custom-call | tf_op jit(solution)/shard_map/pallas_call | solution.py:562

commit v4 on v3

--- a/solution.py
+++ b/solution.py
@@ -383,6 +383,11 @@
         ),
     ]
 
+    late = [
+        remote(mesh_hbm.at[1, pl.ds(14, 2)], left_hbm.at[0], send5.at[2], recv5.at[2], after),
+        remote(mesh_hbm.at[1, pl.ds(0, 2)], right_hbm.at[0], send5.at[3], recv5.at[3], before),
+    ]
+
     gather_members(landed, slot_ref, member)
     for c in range(4):
         loads[c].wait()
@@ -407,10 +412,9 @@
     whole = pltpu.make_async_copy(field.at[pl.ds(2, 16)], part_hbm, stored.at[0])
     whole.start()
     finish(copies)
-    two = pl.ds(1, 2)
-    halos = [
-        remote(mesh_hbm.at[two, pl.ds(14, 2)], left_hbm, send5.at[2], recv5.at[2], after),
-        remote(mesh_hbm.at[two, pl.ds(0, 2)], right_hbm, send5.at[3], recv5.at[3], before),
+    halos = late + [
+        remote(mesh_hbm.at[2, pl.ds(14, 2)], left_hbm.at[1], send5.at[6], recv5.at[6], after),
+        remote(mesh_hbm.at[2, pl.ds(0, 2)], right_hbm.at[1], send5.at[7], recv5.at[7], before),
     ]
 
     scatter(landed2, vertex_ref, values, places, total, inter_ref)
@@ -446,7 +450,7 @@
 
 def smooth_kernel(
     place_ref, inter_ref, edge_ref, part_hbm, mesh_hbm, left_hbm, right_hbm, out_hbm,
-    field, once, arrived, leaving,
+    field, once, swept_part, arrived, leaving,
 ):
     place = place_ref[0]
     has_left, has_right = place > 0, place < 127
@@ -466,8 +470,9 @@
     for k in (1, 2):
         for copy in fetch(k):
             copy.start()
-    done = pltpu.make_async_copy(part_hbm, out_hbm.at[0], leaving.at[0])
-    done.start()
+    early = pltpu.make_async_copy(part_hbm, swept_part, arrived.at[0, 0])
+    early.start()
+    done = pltpu.make_async_copy(swept_part, out_hbm.at[0], leaving.at[0])
     for k in (1, 2):
         finish(fetch(k))
         part = field.at[k - 1]
@@ -477,6 +482,9 @@
         part[18, 0:1, :] = edge_ref[1, k : k + 1, :]
         close_ends(part, has_left, has_right)
         sweep_once(part, once, has_left, has_right)
+        if k == 1:
+            early.wait()
+            done.start()
         sweep_again(part, once)
         store(k).start()
     done.wait()
@@ -547,8 +555,8 @@
             dma((7,)),
             dma((15,)),
             dma((15,)),
-            dma((6,)),
-            dma((6,)),
+            dma((8,)),
+            dma((8,)),
             dma((4,)),
         ],
         compiler_params=pltpu.CompilerParams(
@@ -567,6 +575,7 @@
         scratch_shapes=[
             pltpu.VMEM((2, 20, 96, 512), f32),
             pltpu.VMEM((18, 96, 512), f32),
+            pltpu.VMEM((16, 96, 512), f32),
             pltpu.SemaphoreType.DMA((3, 3)),
             pltpu.SemaphoreType.DMA((3,)),
         ],

time: 146 us -> 61.8 us (0.42)
  Pallas kernels: 146 us -> 61.7 us
    pallas_call x1, Pallas kernels: 97.4 us -> 16.6 us  [smooth(): pl.pallas_call(smooth_kernel, out_shape=jax.ShapeDtypeStruct((3, 16, 96,...]
    pallas_call x1, Pallas kernels: 48.3 us -> 45 us  [transfer(): pl.pallas_call(transfer_kernel, out_shape=(jax.ShapeDtypeStruct((3, 16, 5...]
where the time goes in v4:
time: 61.8 us; the launch traced here: 61.7 us
  Pallas kernels  61.7 us (100%)
    pallas_call x1, Pallas kernels, transfer(): pl.pallas_call(transfer_kernel, out_shape=(jax.ShapeDtypeStruct((3, 16, 5...  45 us
    pallas_call x1, Pallas kernels, smooth(): pl.pallas_call(smooth_kernel, out_shape=jax.ShapeDtypeStruct((3, 16, 96,...  16.6 us

profile of v4, /device:TPU:0, one launch (start us, length us, event | category | flops | bytes accessed | tf_op | source)
XLA Modules:
  0.0 61.7 jit_solution(16379158087228272659)
XLA Ops:
  0.0 45.0 %shard_map.100 = (f32[3,16,512]{2,1,0:T(8,128)}, f32[2,8,512]{2,1,0:T(8,128)}, f32[2,2,96,512]{3,2,1,0:T(8,128)}, f32[2,2,96,512]{3,2,1,0:T(8,128)}, f32[16,96,512]{2,1,0:T(8,128)}) custom-call(f32[3,4096]{1,0:T(4,128)} %disp_hbm.1, s32[64,128]{1,0:T(8,128)} %bitcast.8, s32[4,1024]{1,0:T(4,128)} %slot_hbm.1, f32[3,4,1024]{2,1,0:T(4,128)} %bitcast.6, ...), custom_call_target="tpu_custom_call" | custom-call | tf_op jit(solution)/shard_map/pallas_call | solution.py:518
  45.1 16.6 %shard_map.101 = f32[3,16,96,512]{3,2,1,0:T(8,128)} custom-call(s32[1]{0:T(128)} %bitcast.place_ref, f32[3,16,512]{2,1,0:T(8,128)} %get-tuple-element.10.inter_ref, f32[2,8,512]{2,1,0:T(8,128)} %get-tuple-element.11.edge_ref, f32[16,96,512]{2,1,0:T(8,128)} %get-tuple-element.12.part_hbm, f32[3,16,96,512]{3,2,1,0:T(8,128)} %mesh_hbm.3, ...), custom_call_target="tpu_custom_call" | custom-call | tf_op jit(solution)/shard_map/pallas_call | solution.py:570

commit v5 on v4

--- a/solution.py
+++ b/solution.py
@@ -251,58 +251,55 @@
             )
 
 
-def swept(ref, out_ref, source, target, inside=None):
-    rows = 16
-    lane = lax.broadcasted_iota(jnp.int32, (rows, 512), 1)
-    line = lax.broadcasted_iota(jnp.int32, (rows, 512), 0)
-    for y in range(0, 96, rows):
-        center = ref[source, y : y + rows, :]
-        if y == 0:
-            above = pltpu.roll(center, 1, 0)
-        else:
-            above = ref[source, y - 1 : y - 1 + rows, :]
-        if y + rows == 96:
-            below = jnp.where(line == rows - 1, 0.0, pltpu.roll(center, rows - 1, 0))
-        else:
-            below = ref[source, y + 1 : y + 1 + rows, :]
-        beside = ref[source - 1, y : y + rows, :] + ref[source + 1, y : y + rows, :]
-        beside = beside + (above + below)
-        beside = beside + jnp.where(lane == 0, 0.0, pltpu.roll(center, 1, 1))
-        beside = beside + jnp.where(lane == 511, 0.0, pltpu.roll(center, 511, 1))
-        moved = center * keep_rate + beside * spread_rate
-        if y == 0:
-            moved = jnp.where(line == 0, center, moved)
-        if inside is not None:
-            moved = jnp.where(inside, moved, 0.0)
-        out_ref[target, y : y + rows, :] = moved
-
-
-def sweep_once(field, once, has_left, has_right):
-    def plane(x, carry):
-        swept(field, once, x + 1, x)
-        return carry
-
-    swept(field, once, 1, 0, has_left)
-    lax.fori_loop(1, 17, plane, 0)
-    swept(field, once, 18, 17, has_right)
-
-
-def sweep_again(field, once):
-    def plane(x, carry):
-        swept(once, field, x + 1, x + 2)
-        return carry
-
-    lax.fori_loop(0, 16, plane, 0)
-
-
-def close_ends(field, has_left, has_right):
-    @pl.when(jnp.logical_not(has_left))
+def neighbour_band(band):
+    row = jnp.bitwise_and(lax.broadcasted_iota(jnp.int32, (512, 256), 0), 255)
+    column = lax.broadcasted_iota(jnp.int32, (512, 256), 1)
+    near = (row == column + 1) | (row == column - 1)
+    band[...] = jnp.where(near, 1.0, 0.0).astype(bf16)
+
+
+def clear_margins(field):
+    count = field.shape[1]
+    for q in range(4):
+        for x in range(count):
+            field[q, x, 0:8, :] = jnp.zeros((8, 128), f32)
+            field[q, x, 104:112, :] = jnp.zeros((8, 128), f32)
+
+
+def swept(source, target, band, count, start, place):
+    lane = lax.broadcasted_iota(jnp.int32, (count, 96, 128), 2)
+    line = lax.broadcasted_iota(jnp.int32, (count, 96, 128), 1)
+    here = pl.ds(start, count)
+    center = [source[q, here, 8:104, :] for q in range(4)]
+    upper, lower = [], []
+    for part in center:
+        high = part.astype(bf16)
+        upper.append(high.reshape(count * 96, 128))
+        lower.append((part - high.astype(f32)).astype(bf16).reshape(count * 96, 128))
+    along = []
+    for q in (0, 2):
+        parts = jnp.concatenate([upper[q], upper[q + 1], lower[q], lower[q + 1]], axis=1)
+        along.append(jnp.dot(parts, band[...], preferred_element_type=f32))
+    for q in range(4):
+        beside = along[q // 2][:, 128 * (q % 2) : 128 * (q % 2) + 128].reshape(count, 96, 128)
+        if q == 1:
+            beside = beside + jnp.where(lane == 127, pltpu.roll(center[2], 127, 2), 0.0)
+        if q == 2:
+            beside = beside + jnp.where(lane == 0, pltpu.roll(center[1], 1, 2), 0.0)
+        beside = beside + (source[q, here, 7:103, :] + source[q, here, 9:105, :])
+        beside = beside + (
+            source[q, pl.ds(start - 1, count), 8:104, :]
+            + source[q, pl.ds(start + 1, count), 8:104, :]
+        )
+        moved = center[q] * keep_rate + beside * spread_rate
+        target[q, pl.ds(place, count), 8:104, :] = jnp.where(line == 0, center[q], moved)
+
+
+def close_end(field, x, inside):
+    @pl.when(jnp.logical_not(inside))
     def _():
-        field[1] = jnp.zeros((96, 512), f32)
-
-    @pl.when(jnp.logical_not(has_right))
-    def _():
-        field[18] = jnp.zeros((96, 512), f32)
+        for q in range(4):
+            field[q, x, 8:104, :] = jnp.zeros((96, 128), f32)
 
 
 def add_wall(inter, before, after, field):
@@ -321,7 +318,7 @@
             inter[x : x + 1],
             jnp.where(row == 1, first[x : x + 1], jnp.where(row == 2, second[x : x + 1], 0.0)),
         )
-        field[x + 2, 0:8, :] += extra
+        field[x, 0:8, :] += extra
 
 
 def transfer_kernel(
@@ -331,7 +328,7 @@
     disp_ref, node_ref, slot_ref, source_ref, target_ref, weight_ref, pick_ref, vertex_ref,
     messages, held, ready, landed, messages2, held2, ready2, landed2,
     inverse, member, left, right, upper, lower, result, values, places, total,
-    inter_ref, ends, near, field, once,
+    inter_ref, ends, near, field, once, halo, band,
     fetched, loaded, send1, recv1, send2, recv2, send3, recv3, send4, recv4, send5, recv5, stored,
 ):
     me = lax.axis_index("dev")
@@ -354,7 +351,14 @@
     for peer in peers:
         pl.semaphore_signal(barrier, inc=1, device_id=(peer,), device_id_type=MESH)
     loads = [pltpu.make_async_copy(inv_hbm.at[c], inverse.at[c], loaded.at[c]) for c in range(4)]
-    loads.append(pltpu.make_async_copy(mesh_hbm.at[0], field.at[pl.ds(2, 16)], loaded.at[4]))
+    loads += [
+        pltpu.make_async_copy(
+            mesh_hbm.at[0, :, :, pl.ds(128 * q, 128)],
+            field.at[q, pl.ds(2, 16), pl.ds(8, 96)],
+            loaded.at[4 + q],
+        )
+        for q in range(4)
+    ]
     for load in loads:
         load.start()
 
@@ -366,6 +370,9 @@
 
     copies = first_stage(messages, held, send1, recv1, outer, inner)
     finish(fetches[2:])
+    neighbour_band(band)
+    clear_margins(field)
+    clear_margins(once)
     exponent_rows(source_ref, target_ref, left, right)
     kernel_values(0, left, right, upper, lower)
     kernel_values(1, left, right, upper, lower)
@@ -375,14 +382,9 @@
     kernel_values(3, left, right, upper, lower)
     finish(copies)
     halos = [
-        remote(
-            mesh_hbm.at[0, pl.ds(14, 2)], field.at[pl.ds(0, 2)], send5.at[0], recv5.at[0], after
-        ),
-        remote(
-            mesh_hbm.at[0, pl.ds(0, 2)], field.at[pl.ds(18, 2)], send5.at[1], recv5.at[1], before
-        ),
-    ]
-
+        remote(mesh_hbm.at[0, pl.ds(14, 2)], halo.at[0], send5.at[0], recv5.at[0], after),
+        remote(mesh_hbm.at[0, pl.ds(0, 2)], halo.at[1], send5.at[1], recv5.at[1], before),
+    ]
     late = [
         remote(mesh_hbm.at[1, pl.ds(14, 2)], left_hbm.at[0], send5.at[2], recv5.at[2], after),
         remote(mesh_hbm.at[1, pl.ds(0, 2)], right_hbm.at[0], send5.at[3], recv5.at[3], before),
@@ -397,20 +399,36 @@
         lambda k, r: result[r // 8, k : k + 1, (r % 8) * 128 : (r % 8 + 1) * 128],
         messages2,
     )
-    loads[4].wait()
+    finish(loads[4:])
     copies = first_stage(messages2, held2, send3, recv3, outer, inner)
     finish(halos)
-    field[1, 0:1, :] = jnp.zeros((1, 512), f32)
-    field[18, 0:1, :] = jnp.zeros((1, 512), f32)
-    for x in range(16):
-        field[x + 2, 0:1, :] = jnp.zeros((1, 512), f32)
-    close_ends(field, has_left, has_right)
-    sweep_once(field, once, has_left, has_right)
+    for q in range(4):
+        lanes = slice(128 * q, 128 * (q + 1))
+        for side in range(2):
+            for x in range(2):
+                field[q, 18 * side + x, 8:104, :] = halo[side, x, :, lanes]
+        for x in range(1, 19):
+            field[q, x, 8:9, :] = jnp.zeros((1, 128), f32)
+    close_end(field, 1, has_left)
+    close_end(field, 18, has_right)
+    for i in range(2):
+        swept(field, once, band, 9, 9 * i + 1, 9 * i)
+    close_end(once, 0, has_left)
+    close_end(once, 17, has_right)
     finish(copies)
     copies = second_stage(held2, ready2, landed2, send4, recv4, outer, inner)
-    sweep_again(field, once)
-    whole = pltpu.make_async_copy(field.at[pl.ds(2, 16)], part_hbm, stored.at[0])
-    whole.start()
+    for i in range(2):
+        swept(once, field, band, 8, 8 * i + 1, 8 * i + 2)
+    whole = [
+        pltpu.make_async_copy(
+            field.at[q, pl.ds(2, 16), pl.ds(8, 96)],
+            part_hbm.at[:, :, pl.ds(128 * q, 128)],
+            stored.at[q],
+        )
+        for q in range(4)
+    ]
+    for copy in whole:
+        copy.start()
     finish(copies)
     halos = late + [
         remote(mesh_hbm.at[2, pl.ds(14, 2)], left_hbm.at[1], send5.at[6], recv5.at[6], after),
@@ -426,70 +444,97 @@
         remote(ends.at[1], near.at[0], send5.at[4], recv5.at[4], after),
         remote(ends.at[0], near.at[1], send5.at[5], recv5.at[5], before),
     ]
-    wall = pltpu.make_async_copy(inter_ref, inter_hbm, stored.at[1])
+    wall = pltpu.make_async_copy(inter_ref, inter_hbm, stored.at[4])
     wall.start()
-    whole.wait()
     finish(edges)
-    edge = pltpu.make_async_copy(near, edge_hbm, stored.at[2])
+    edge = pltpu.make_async_copy(near, edge_hbm, stored.at[5])
     edge.start()
-    add_wall(
-        inter_ref[0],
-        jnp.where(has_left, near[0, 0:1, :], 0.0),
-        jnp.where(has_right, near[1, 0:1, :], 0.0),
-        field,
-    )
-    rows = pltpu.make_async_copy(
-        field.at[pl.ds(2, 16), pl.ds(0, 8)], part_hbm.at[:, pl.ds(0, 8)], stored.at[3]
-    )
-    rows.start()
+    finish(whole)
     wall.wait()
     edge.wait()
-    rows.wait()
     finish(halos)
 
 
 def smooth_kernel(
     place_ref, inter_ref, edge_ref, part_hbm, mesh_hbm, left_hbm, right_hbm, out_hbm,
-    field, once, swept_part, arrived, leaving,
+    field, once, swept_part, band, arrived, leaving,
 ):
     place = place_ref[0]
     has_left, has_right = place > 0, place < 127
 
-    def fetch(k):
-        return (
-            pltpu.make_async_copy(left_hbm.at[k - 1], field.at[k - 1, pl.ds(0, 2)], arrived.at[k, 0]),
-            pltpu.make_async_copy(mesh_hbm.at[k], field.at[k - 1, pl.ds(2, 16)], arrived.at[k, 1]),
+    def fetch(k, half):
+        first, count = ((0, 9), (9, 7))[half]
+        side, at = ((left_hbm, 0), (right_hbm, 18))[half]
+        copies = []
+        for q in range(4):
+            lanes = pl.ds(128 * q, 128)
+            copies.append(
+                pltpu.make_async_copy(
+                    mesh_hbm.at[k, pl.ds(first, count), :, lanes],
+                    field.at[k - 1, q, pl.ds(first + 2, count), pl.ds(8, 96)],
+                    arrived.at[k, half, q, 0],
+                )
+            )
+            copies.append(
+                pltpu.make_async_copy(
+                    side.at[k - 1, :, :, lanes],
+                    field.at[k - 1, q, pl.ds(at, 2), pl.ds(8, 96)],
+                    arrived.at[k, half, q, 1],
+                )
+            )
+        return copies
+
+    def store(k, half):
+        return [
             pltpu.make_async_copy(
-                right_hbm.at[k - 1], field.at[k - 1, pl.ds(18, 2)], arrived.at[k, 2]
-            ),
-        )
-
-    def store(k):
-        return pltpu.make_async_copy(field.at[k - 1, pl.ds(2, 16)], out_hbm.at[k], leaving.at[k])
+                field.at[k - 1, q, pl.ds(2 + 8 * half, 8), pl.ds(8, 96)],
+                out_hbm.at[k, pl.ds(8 * half, 8), :, pl.ds(128 * q, 128)],
+                leaving.at[k, half, q],
+            )
+            for q in range(4)
+        ]
 
     for k in (1, 2):
-        for copy in fetch(k):
-            copy.start()
-    early = pltpu.make_async_copy(part_hbm, swept_part, arrived.at[0, 0])
+        for half in range(2):
+            for copy in fetch(k, half):
+                copy.start()
+    early = pltpu.make_async_copy(part_hbm, swept_part, arrived.at[0, 0, 0, 0])
     early.start()
-    done = pltpu.make_async_copy(swept_part, out_hbm.at[0], leaving.at[0])
+    done = pltpu.make_async_copy(swept_part, out_hbm.at[0], leaving.at[0, 0, 0])
+    neighbour_band(band)
+    clear_margins(once)
     for k in (1, 2):
-        finish(fetch(k))
         part = field.at[k - 1]
-        for x in range(16):
-            part[x + 2, 0:1, :] = inter_ref[k, x : x + 1, :]
-        part[1, 0:1, :] = edge_ref[0, k : k + 1, :]
-        part[18, 0:1, :] = edge_ref[1, k : k + 1, :]
-        close_ends(part, has_left, has_right)
-        sweep_once(part, once, has_left, has_right)
+        clear_margins(part)
+        for half in range(2):
+            finish(fetch(k, half))
+            for q in range(4):
+                lanes = slice(128 * q, 128 * (q + 1))
+                for x in range(9 * half, 9 + 7 * half):
+                    part[q, x + 2, 8:9, :] = inter_ref[k, x : x + 1, lanes]
+                end = 1 + 17 * half
+                part[q, end, 8:9, :] = edge_ref[half, k : k + 1, lanes]
+            close_end(part, 1 + 17 * half, (has_left, has_right)[half])
+            swept(part, once, band, 9, 9 * half + 1, 9 * half)
+        close_end(once, 0, has_left)
+        close_end(once, 17, has_right)
         if k == 1:
             early.wait()
+            add_wall(
+                inter_ref[0],
+                jnp.where(has_left, edge_ref[0, 0:1, :], 0.0),
+                jnp.where(has_right, edge_ref[1, 0:1, :], 0.0),
+                swept_part,
+            )
             done.start()
-        sweep_again(part, once)
-        store(k).start()
+        for half in range(2):
+            swept(once, part, band, 8, 8 * half + 1, 8 * half + 2)
+            for copy in store(k, half):
+                copy.start()
     done.wait()
     for k in (1, 2):
-        store(k).wait()
+        for half in range(2):
+            finish(store(k, half))
 
 
 def transfer(
@@ -543,10 +588,12 @@
             pltpu.VMEM((3, 16, 512), f32),
             pltpu.VMEM((2, 8, 512), f32),
             pltpu.VMEM((2, 8, 512), f32),
-            pltpu.VMEM((20, 96, 512), f32),
-            pltpu.VMEM((18, 96, 512), f32),
+            pltpu.VMEM((4, 20, 112, 128), f32),
+            pltpu.VMEM((4, 18, 112, 128), f32),
+            pltpu.VMEM((2, 2, 96, 512), f32),
+            pltpu.VMEM((512, 256), bf16),
             dma((8,)),
-            dma((5,)),
+            dma((8,)),
             dma((7,)),
             dma((7,)),
             dma((15,)),
@@ -557,7 +604,7 @@
             dma((15,)),
             dma((8,)),
             dma((8,)),
-            dma((4,)),
+            dma((6,)),
         ],
         compiler_params=pltpu.CompilerParams(
             collective_id=1, has_side_effects=True, vmem_limit_bytes=63 << 20
@@ -573,11 +620,12 @@
         in_specs=[pl.BlockSpec(memory_space=pltpu.SMEM), vmem(), vmem(), hbm, hbm, hbm, hbm],
         out_specs=hbm,
         scratch_shapes=[
-            pltpu.VMEM((2, 20, 96, 512), f32),
-            pltpu.VMEM((18, 96, 512), f32),
+            pltpu.VMEM((2, 4, 20, 112, 128), f32),
+            pltpu.VMEM((4, 18, 112, 128), f32),
             pltpu.VMEM((16, 96, 512), f32),
-            pltpu.SemaphoreType.DMA((3, 3)),
-            pltpu.SemaphoreType.DMA((3,)),
+            pltpu.VMEM((512, 256), bf16),
+            pltpu.SemaphoreType.DMA((3, 2, 4, 2)),
+            pltpu.SemaphoreType.DMA((3, 2, 4)),
         ],
         compiler_params=pltpu.CompilerParams(vmem_limit_bytes=63 << 20),
     )(place, interface, edges, part, mesh_before, left, right)

time: 61.8 us -> 58.4 us (0.945)
  Pallas kernels: 61.7 us -> 58.1 us
    pallas_call x1, Pallas kernels: 16.6 us -> 13.2 us  [smooth(): pl.pallas_call(smooth_kernel, out_shape=jax.ShapeDtypeStruct((3, 16, 96,...]
where the time goes in v5:
time: 58.4 us; the launch traced here: 58.2 us
  Pallas kernels  58.1 us (99%)
    pallas_call x1, Pallas kernels, transfer(): pl.pallas_call(transfer_kernel, out_shape=(jax.ShapeDtypeStruct((3, 16, 5...  44.8 us
    pallas_call x1, Pallas kernels, smooth(): pl.pallas_call(smooth_kernel, out_shape=jax.ShapeDtypeStruct((3, 16, 96,...  13.2 us

profile of v5, /device:TPU:0, one launch (start us, length us, event | category | flops | bytes accessed | tf_op | source)
XLA Modules:
  0.0 58.2 jit_solution(2921622340084154748)
XLA Ops:
  0.0 44.8 %shard_map.100 = (f32[3,16,512]{2,1,0:T(8,128)}, f32[2,8,512]{2,1,0:T(8,128)}, f32[2,2,96,512]{3,2,1,0:T(8,128)}, f32[2,2,96,512]{3,2,1,0:T(8,128)}, f32[16,96,512]{2,1,0:T(8,128)}) custom-call(f32[3,4096]{1,0:T(4,128)} %disp_hbm.1, s32[64,128]{1,0:T(8,128)} %bitcast.8, s32[4,1024]{1,0:T(4,128)} %slot_hbm.1, f32[3,4,1024]{2,1,0:T(4,128)} %bitcast.6, ...), custom_call_target="tpu_custom_call" | custom-call | tf_op jit(solution)/shard_map/pallas_call | solution.py:563
  44.8 13.2 %shard_map.101 = f32[3,16,96,512]{3,2,1,0:T(8,128)} custom-call(s32[1]{0:T(128)} %bitcast.place_ref, f32[3,16,512]{2,1,0:T(8,128)} %get-tuple-element.10.inter_ref, f32[2,8,512]{2,1,0:T(8,128)} %get-tuple-element.11.edge_ref, f32[16,96,512]{2,1,0:T(8,128)} %get-tuple-element.12.part_hbm, f32[3,16,96,512]{3,2,1,0:T(8,128)} %mesh_hbm.3, ...), custom_call_target="tpu_custom_call" | custom-call | tf_op jit(solution)/shard_map/pallas_call | solution.py:617

commit v6 on v5

--- a/solution.py
+++ b/solution.py
@@ -302,6 +302,24 @@
             field[q, x, 8:104, :] = jnp.zeros((96, 128), f32)
 
 
+def sweep_open(field, once, halo, band, has_left, has_right):
+    for q in range(4):
+        lanes = slice(128 * q, 128 * (q + 1))
+        for side in range(2):
+            for x in range(2):
+                field[q, 18 * side + x, 8:104, :] = halo[side, x, :, lanes]
+        for x in range(1, 19):
+            field[q, x, 8:9, :] = jnp.zeros((1, 128), f32)
+    close_end(field, 1, has_left)
+    close_end(field, 18, has_right)
+    for i in range(2):
+        swept(field, once, band, 9, 9 * i + 1, 9 * i)
+    close_end(once, 0, has_left)
+    close_end(once, 17, has_right)
+    for i in range(2):
+        swept(once, field, band, 8, 8 * i + 1, 8 * i + 2)
+
+
 def add_wall(inter, before, after, field):
     lane = lax.broadcasted_iota(jnp.int32, (16, 512), 1)
     line = lax.broadcasted_iota(jnp.int32, (16, 512), 0)
@@ -353,10 +371,11 @@
     loads = [pltpu.make_async_copy(inv_hbm.at[c], inverse.at[c], loaded.at[c]) for c in range(4)]
     loads += [
         pltpu.make_async_copy(
-            mesh_hbm.at[0, :, :, pl.ds(128 * q, 128)],
-            field.at[q, pl.ds(2, 16), pl.ds(8, 96)],
-            loaded.at[4 + q],
-        )
+            mesh_hbm.at[k, :, :, pl.ds(128 * q, 128)],
+            field.at[k, q, pl.ds(2, 16), pl.ds(8, 96)],
+            loaded.at[4 + 4 * k + q],
+        )
+        for k in range(2)
         for q in range(4)
     ]
     for load in loads:
@@ -371,7 +390,8 @@
     copies = first_stage(messages, held, send1, recv1, outer, inner)
     finish(fetches[2:])
     neighbour_band(band)
-    clear_margins(field)
+    clear_margins(field.at[0])
+    clear_margins(field.at[1])
     clear_margins(once)
     exponent_rows(source_ref, target_ref, left, right)
     kernel_values(0, left, right, upper, lower)
@@ -381,14 +401,18 @@
     kernel_values(2, left, right, upper, lower)
     kernel_values(3, left, right, upper, lower)
     finish(copies)
-    halos = [
-        remote(mesh_hbm.at[0, pl.ds(14, 2)], halo.at[0], send5.at[0], recv5.at[0], after),
-        remote(mesh_hbm.at[0, pl.ds(0, 2)], halo.at[1], send5.at[1], recv5.at[1], before),
-    ]
-    late = [
-        remote(mesh_hbm.at[1, pl.ds(14, 2)], left_hbm.at[0], send5.at[2], recv5.at[2], after),
-        remote(mesh_hbm.at[1, pl.ds(0, 2)], right_hbm.at[0], send5.at[3], recv5.at[3], before),
-    ]
+    halos = []
+    for k in range(2):
+        halos += [
+            remote(
+                mesh_hbm.at[k, pl.ds(14, 2)], halo.at[k, 0],
+                send5.at[2 * k], recv5.at[2 * k], after,
+            ),
+            remote(
+                mesh_hbm.at[k, pl.ds(0, 2)], halo.at[k, 1],
+                send5.at[2 * k + 1], recv5.at[2 * k + 1], before,
+            ),
+        ]
 
     gather_members(landed, slot_ref, member)
     for c in range(4):
@@ -401,38 +425,27 @@
     )
     finish(loads[4:])
     copies = first_stage(messages2, held2, send3, recv3, outer, inner)
-    finish(halos)
-    for q in range(4):
-        lanes = slice(128 * q, 128 * (q + 1))
-        for side in range(2):
-            for x in range(2):
-                field[q, 18 * side + x, 8:104, :] = halo[side, x, :, lanes]
-        for x in range(1, 19):
-            field[q, x, 8:9, :] = jnp.zeros((1, 128), f32)
-    close_end(field, 1, has_left)
-    close_end(field, 18, has_right)
-    for i in range(2):
-        swept(field, once, band, 9, 9 * i + 1, 9 * i)
-    close_end(once, 0, has_left)
-    close_end(once, 17, has_right)
+    finish(halos[:2])
+    sweep_open(field.at[0], once, halo.at[0], band, has_left, has_right)
     finish(copies)
     copies = second_stage(held2, ready2, landed2, send4, recv4, outer, inner)
-    for i in range(2):
-        swept(once, field, band, 8, 8 * i + 1, 8 * i + 2)
+    finish(halos[2:])
+    sweep_open(field.at[1], once, halo.at[1], band, has_left, has_right)
     whole = [
         pltpu.make_async_copy(
-            field.at[q, pl.ds(2, 16), pl.ds(8, 96)],
-            part_hbm.at[:, :, pl.ds(128 * q, 128)],
-            stored.at[q],
-        )
+            field.at[k, q, pl.ds(2, 16), pl.ds(8, 96)],
+            part_hbm.at[k, :, :, pl.ds(128 * q, 128)],
+            stored.at[4 * k + q],
+        )
+        for k in range(2)
         for q in range(4)
     ]
     for copy in whole:
         copy.start()
     finish(copies)
-    halos = late + [
-        remote(mesh_hbm.at[2, pl.ds(14, 2)], left_hbm.at[1], send5.at[6], recv5.at[6], after),
-        remote(mesh_hbm.at[2, pl.ds(0, 2)], right_hbm.at[1], send5.at[7], recv5.at[7], before),
+    halos = [
+        remote(mesh_hbm.at[2, pl.ds(14, 2)], left_hbm, send5.at[6], recv5.at[6], after),
+        remote(mesh_hbm.at[2, pl.ds(0, 2)], right_hbm, send5.at[7], recv5.at[7], before),
     ]
 
     scatter(landed2, vertex_ref, values, places, total, inter_ref)
@@ -444,10 +457,10 @@
         remote(ends.at[1], near.at[0], send5.at[4], recv5.at[4], after),
         remote(ends.at[0], near.at[1], send5.at[5], recv5.at[5], before),
     ]
-    wall = pltpu.make_async_copy(inter_ref, inter_hbm, stored.at[4])
+    wall = pltpu.make_async_copy(inter_ref, inter_hbm, stored.at[8])
     wall.start()
     finish(edges)
-    edge = pltpu.make_async_copy(near, edge_hbm, stored.at[5])
+    edge = pltpu.make_async_copy(near, edge_hbm, stored.at[9])
     edge.start()
     finish(whole)
     wall.wait()
@@ -457,12 +470,12 @@
 
 def smooth_kernel(
     place_ref, inter_ref, edge_ref, part_hbm, mesh_hbm, left_hbm, right_hbm, out_hbm,
-    field, once, swept_part, band, arrived, leaving,
+    field, once, opened, band, arrived, arrived_open, leaving, leaving_open,
 ):
     place = place_ref[0]
     has_left, has_right = place > 0, place < 127
 
-    def fetch(k, half):
+    def fetch(half):
         first, count = ((0, 9), (9, 7))[half]
         side, at = ((left_hbm, 0), (right_hbm, 18))[half]
         copies = []
@@ -470,71 +483,69 @@
             lanes = pl.ds(128 * q, 128)
             copies.append(
                 pltpu.make_async_copy(
-                    mesh_hbm.at[k, pl.ds(first, count), :, lanes],
-                    field.at[k - 1, q, pl.ds(first + 2, count), pl.ds(8, 96)],
-                    arrived.at[k, half, q, 0],
+                    mesh_hbm.at[2, pl.ds(first, count), :, lanes],
+                    field.at[q, pl.ds(first + 2, count), pl.ds(8, 96)],
+                    arrived.at[half, q, 0],
                 )
             )
             copies.append(
                 pltpu.make_async_copy(
-                    side.at[k - 1, :, :, lanes],
-                    field.at[k - 1, q, pl.ds(at, 2), pl.ds(8, 96)],
-                    arrived.at[k, half, q, 1],
+                    side.at[:, :, lanes],
+                    field.at[q, pl.ds(at, 2), pl.ds(8, 96)],
+                    arrived.at[half, q, 1],
                 )
             )
         return copies
 
-    def store(k, half):
+    def store(half):
         return [
             pltpu.make_async_copy(
-                field.at[k - 1, q, pl.ds(2 + 8 * half, 8), pl.ds(8, 96)],
-                out_hbm.at[k, pl.ds(8 * half, 8), :, pl.ds(128 * q, 128)],
-                leaving.at[k, half, q],
+                field.at[q, pl.ds(2 + 8 * half, 8), pl.ds(8, 96)],
+                out_hbm.at[2, pl.ds(8 * half, 8), :, pl.ds(128 * q, 128)],
+                leaving.at[half, q],
             )
             for q in range(4)
         ]
 
-    for k in (1, 2):
-        for half in range(2):
-            for copy in fetch(k, half):
-                copy.start()
-    early = pltpu.make_async_copy(part_hbm, swept_part, arrived.at[0, 0, 0, 0])
-    early.start()
-    done = pltpu.make_async_copy(swept_part, out_hbm.at[0], leaving.at[0, 0, 0])
+    arriving = [fetch(0), fetch(1)]
+    for copy in arriving[0] + arriving[1]:
+        copy.start()
+    early = [
+        pltpu.make_async_copy(part_hbm.at[k], opened.at[k], arrived_open.at[k]) for k in range(2)
+    ]
+    for copy in early:
+        copy.start()
+    stores = [
+        pltpu.make_async_copy(opened.at[k], out_hbm.at[k], leaving_open.at[k]) for k in range(2)
+    ]
     neighbour_band(band)
     clear_margins(once)
-    for k in (1, 2):
-        part = field.at[k - 1]
-        clear_margins(part)
-        for half in range(2):
-            finish(fetch(k, half))
-            for q in range(4):
-                lanes = slice(128 * q, 128 * (q + 1))
-                for x in range(9 * half, 9 + 7 * half):
-                    part[q, x + 2, 8:9, :] = inter_ref[k, x : x + 1, lanes]
-                end = 1 + 17 * half
-                part[q, end, 8:9, :] = edge_ref[half, k : k + 1, lanes]
-            close_end(part, 1 + 17 * half, (has_left, has_right)[half])
-            swept(part, once, band, 9, 9 * half + 1, 9 * half)
-        close_end(once, 0, has_left)
-        close_end(once, 17, has_right)
-        if k == 1:
-            early.wait()
-            add_wall(
-                inter_ref[0],
-                jnp.where(has_left, edge_ref[0, 0:1, :], 0.0),
-                jnp.where(has_right, edge_ref[1, 0:1, :], 0.0),
-                swept_part,
-            )
-            done.start()
-        for half in range(2):
-            swept(once, part, band, 8, 8 * half + 1, 8 * half + 2)
-            for copy in store(k, half):
-                copy.start()
-    done.wait()
-    for k in (1, 2):
-        for half in range(2):
-            finish(store(k, half))
+    clear_margins(field)
+    for half in range(2):
+        finish(arriving[half])
+        for q in range(4):
+            lanes = slice(128 * q, 128 * (q + 1))
+            for x in range(9 * half, 9 + 7 * half):
+                field[q, x + 2, 8:9, :] = inter_ref[2, x : x + 1, lanes]
+            field[q, 1 + 17 * half, 8:9, :] = edge_ref[half, 2:3, lanes]
+        close_end(field, 1 + 17 * half, (has_left, has_right)[half])
+        swept(field, once, band, 9, 9 * half + 1, 9 * half)
+        early[half].wait()
+        add_wall(
+            inter_ref[half],
+            jnp.where(has_left, edge_ref[0, half : half + 1, :], 0.0),
+            jnp.where(has_right, edge_ref[1, half : half + 1, :], 0.0),
+            opened.at[half],
+        )
+        stores[half].start()
+    close_end(once, 0, has_left)
+    close_end(once, 17, has_right)
+    for half in range(2):
+        swept(once, field, band, 8, 8 * half + 1, 8 * half + 2)
+        stores += store(half)
+        for copy in stores[-4:]:
+            copy.start()
+    finish(stores)
 
 
 def transfer(
@@ -543,7 +554,7 @@
 ):
     hbm = pl.BlockSpec(memory_space=pl.ANY)
     dma = pltpu.SemaphoreType.DMA
-    halo = jax.ShapeDtypeStruct((2, 2, 96, 512), f32)
+    halo = jax.ShapeDtypeStruct((2, 96, 512), f32)
     exchange = [
         pltpu.VMEM((192, 128), f32),
         pltpu.VMEM((192, 128), f32),
@@ -567,7 +578,7 @@
             jax.ShapeDtypeStruct((2, 8, 512), f32),
             halo,
             halo,
-            jax.ShapeDtypeStruct((16, 96, 512), f32),
+            jax.ShapeDtypeStruct((2, 16, 96, 512), f32),
         ),
         in_specs=[hbm] * 10,
         out_specs=(hbm,) * 5,
@@ -588,12 +599,12 @@
             pltpu.VMEM((3, 16, 512), f32),
             pltpu.VMEM((2, 8, 512), f32),
             pltpu.VMEM((2, 8, 512), f32),
-            pltpu.VMEM((4, 20, 112, 128), f32),
+            pltpu.VMEM((2, 4, 20, 112, 128), f32),
             pltpu.VMEM((4, 18, 112, 128), f32),
-            pltpu.VMEM((2, 2, 96, 512), f32),
+            pltpu.VMEM((2, 2, 2, 96, 512), f32),
             pltpu.VMEM((512, 256), bf16),
             dma((8,)),
-            dma((8,)),
+            dma((12,)),
             dma((7,)),
             dma((7,)),
             dma((15,)),
@@ -604,7 +615,7 @@
             dma((15,)),
             dma((8,)),
             dma((8,)),
-            dma((6,)),
+            dma((10,)),
         ],
         compiler_params=pltpu.CompilerParams(
             collective_id=1, has_side_effects=True, vmem_limit_bytes=63 << 20
@@ -620,12 +631,14 @@
         in_specs=[pl.BlockSpec(memory_space=pltpu.SMEM), vmem(), vmem(), hbm, hbm, hbm, hbm],
         out_specs=hbm,
         scratch_shapes=[
-            pltpu.VMEM((2, 4, 20, 112, 128), f32),
+            pltpu.VMEM((4, 20, 112, 128), f32),
             pltpu.VMEM((4, 18, 112, 128), f32),
-            pltpu.VMEM((16, 96, 512), f32),
+            pltpu.VMEM((2, 16, 96, 512), f32),
             pltpu.VMEM((512, 256), bf16),
-            pltpu.SemaphoreType.DMA((3, 2, 4, 2)),
-            pltpu.SemaphoreType.DMA((3, 2, 4)),
+            pltpu.SemaphoreType.DMA((2, 4, 2)),
+            pltpu.SemaphoreType.DMA((2,)),
+            pltpu.SemaphoreType.DMA((2, 4)),
+            pltpu.SemaphoreType.DMA((2,)),
         ],
         compiler_params=pltpu.CompilerParams(vmem_limit_bytes=63 << 20),
     )(place, interface, edges, part, mesh_before, left, right)

time: 58.4 us -> 55.4 us (0.949)
  Pallas kernels: 58.1 us -> 55.1 us
    pallas_call x1, Pallas kernels: 13.2 us -> 8.73 us  [smooth(): pl.pallas_call(smooth_kernel, out_shape=jax.ShapeDtypeStruct((3, 16, 96,...]
    pallas_call x1, Pallas kernels: 44.8 us -> 46.4 us  [transfer(): pl.pallas_call(transfer_kernel, out_shape=(jax.ShapeDtypeStruct((3, 16, 5...]
where the time goes in v6:
time: 55.4 us; the launch traced here: 55.3 us
  Pallas kernels  55.1 us (99%)
    pallas_call x1, Pallas kernels, transfer(): pl.pallas_call(transfer_kernel, out_shape=(jax.ShapeDtypeStruct((3, 16, 5...  46.4 us
    pallas_call x1, Pallas kernels, smooth(): pl.pallas_call(smooth_kernel, out_shape=jax.ShapeDtypeStruct((3, 16, 96,...  8.73 us

profile of v6, /device:TPU:0, one launch (start us, length us, event | category | flops | bytes accessed | tf_op | source)
XLA Modules:
  0.0 55.3 jit_solution(17710510615817879374)
XLA Ops:
  0.0 46.4 %shard_map.100 = (f32[3,16,512]{2,1,0:T(8,128)}, f32[2,8,512]{2,1,0:T(8,128)}, f32[2,96,512]{2,1,0:T(8,128)}, f32[2,96,512]{2,1,0:T(8,128)}, f32[2,16,96,512]{3,2,1,0:T(8,128)}) custom-call(f32[3,4096]{1,0:T(4,128)} %disp_hbm.1, s32[64,128]{1,0:T(8,128)} %bitcast.8, s32[4,1024]{1,0:T(4,128)} %slot_hbm.1, f32[3,4,1024]{2,1,0:T(4,128)} %bitcast.6, ...), custom_call_target="tpu_custom_call" | custom-call | tf_op jit(solution)/shard_map/pallas_call | solution.py:574
  46.4 8.7 %shard_map.101 = f32[3,16,96,512]{3,2,1,0:T(8,128)} custom-call(s32[1]{0:T(128)} %bitcast.place_ref, f32[3,16,512]{2,1,0:T(8,128)} %get-tuple-element.10.inter_ref, f32[2,8,512]{2,1,0:T(8,128)} %get-tuple-element.11.edge_ref, f32[2,16,96,512]{3,2,1,0:T(8,128)} %get-tuple-element.12.part_hbm, f32[3,16,96,512]{3,2,1,0:T(8,128)} %mesh_hbm.3, ...), custom_call_target="tpu_custom_call" | custom-call | tf_op jit(solution)/shard_map/pallas_call | solution.py:628

commit v7 on v6

--- a/solution.py
+++ b/solution.py
@@ -121,6 +121,44 @@
         )
     landed[outer] = ready[outer]
     return copies
+
+
+def shift(source_last, source_first, left, right, send, receive, me):
+    has_left, has_right = me > 0, me < 127
+
+    def descriptor(source, target, i, device):
+        return pltpu.make_async_remote_copy(
+            src_ref=source,
+            dst_ref=target,
+            send_sem=send[i],
+            recv_sem=receive[i],
+            device_id=(device,),
+            device_id_type=MESH,
+        )
+
+    ahead = descriptor(source_last, left, 0, (me + 1) % 128)
+    back = descriptor(source_first, right, 1, (me + 127) % 128)
+
+    @pl.when(has_right)
+    def _():
+        ahead.start()
+
+    @pl.when(has_left)
+    def _():
+        back.start()
+
+    def wait():
+        @pl.when(has_right)
+        def _():
+            ahead.wait_send()
+            back.wait_recv()
+
+        @pl.when(has_left)
+        def _():
+            back.wait_send()
+            ahead.wait_recv()
+
+    return wait
 
 
 def finish(copies):
@@ -362,6 +400,18 @@
     fetches = [pltpu.make_async_copy(a, b, fetched.at[i]) for i, (a, b) in enumerate(small)]
     for fetch in fetches:
         fetch.start()
+    @pl.when(jnp.logical_not(has_left))
+    def _():
+        near[0] = jnp.zeros((8, 512), f32)
+        for k in range(2):
+            halo[k, 0] = jnp.zeros((2, 96, 512), f32)
+
+    @pl.when(jnp.logical_not(has_right))
+    def _():
+        near[1] = jnp.zeros((8, 512), f32)
+        for k in range(2):
+            halo[k, 1] = jnp.zeros((2, 96, 512), f32)
+
     barrier = pltpu.get_barrier_semaphore()
     peers = [outer * 8 + (inner + i) % 8 for i in range(1, 8)]
     peers += [((outer + i) % 16) * 8 + inner for i in range(1, 16)]
@@ -398,21 +448,23 @@
     kernel_values(1, left, right, upper, lower)
     finish(copies)
     copies = second_stage(held, ready, landed, send2, recv2, outer, inner)
+
+    def send_halo(k):
+        return shift(
+            mesh_hbm.at[k, pl.ds(14, 2)],
+            mesh_hbm.at[k, pl.ds(0, 2)],
+            halo.at[k, 0] if k < 2 else left_hbm,
+            halo.at[k, 1] if k < 2 else right_hbm,
+            (send5.at[2 * k], send5.at[2 * k + 1]),
+            (recv5.at[2 * k], recv5.at[2 * k + 1]),
+            me,
+        )
+
+    halo_waits = [send_halo(0)]
     kernel_values(2, left, right, upper, lower)
     kernel_values(3, left, right, upper, lower)
     finish(copies)
-    halos = []
-    for k in range(2):
-        halos += [
-            remote(
-                mesh_hbm.at[k, pl.ds(14, 2)], halo.at[k, 0],
-                send5.at[2 * k], recv5.at[2 * k], after,
-            ),
-            remote(
-                mesh_hbm.at[k, pl.ds(0, 2)], halo.at[k, 1],
-                send5.at[2 * k + 1], recv5.at[2 * k + 1], before,
-            ),
-        ]
+    halo_waits.append(send_halo(1))
 
     gather_members(landed, slot_ref, member)
     for c in range(4):
@@ -425,11 +477,11 @@
     )
     finish(loads[4:])
     copies = first_stage(messages2, held2, send3, recv3, outer, inner)
-    finish(halos[:2])
+    halo_waits[0]()
     sweep_open(field.at[0], once, halo.at[0], band, has_left, has_right)
     finish(copies)
     copies = second_stage(held2, ready2, landed2, send4, recv4, outer, inner)
-    finish(halos[2:])
+    halo_waits[1]()
     sweep_open(field.at[1], once, halo.at[1], band, has_left, has_right)
     whole = [
         pltpu.make_async_copy(
@@ -443,29 +495,31 @@
     for copy in whole:
         copy.start()
     finish(copies)
-    halos = [
-        remote(mesh_hbm.at[2, pl.ds(14, 2)], left_hbm, send5.at[6], recv5.at[6], after),
-        remote(mesh_hbm.at[2, pl.ds(0, 2)], right_hbm, send5.at[7], recv5.at[7], before),
-    ]
+    halo_waits.append(send_halo(2))
 
     scatter(landed2, vertex_ref, values, places, total, inter_ref)
     ends[...] = jnp.zeros_like(ends)
     for k in range(3):
         ends[0, k : k + 1, :] = inter_ref[k, 0:1, :]
         ends[1, k : k + 1, :] = inter_ref[k, 15:16, :]
-    edges = [
-        remote(ends.at[1], near.at[0], send5.at[4], recv5.at[4], after),
-        remote(ends.at[0], near.at[1], send5.at[5], recv5.at[5], before),
-    ]
+    edge_wait = shift(
+        ends.at[1],
+        ends.at[0],
+        near.at[0],
+        near.at[1],
+        (send5.at[6], send5.at[7]),
+        (recv5.at[6], recv5.at[7]),
+        me,
+    )
     wall = pltpu.make_async_copy(inter_ref, inter_hbm, stored.at[8])
     wall.start()
-    finish(edges)
+    edge_wait()
     edge = pltpu.make_async_copy(near, edge_hbm, stored.at[9])
     edge.start()
     finish(whole)
     wall.wait()
     edge.wait()
-    finish(halos)
+    halo_waits[2]()
 
 
 def smooth_kernel(

time: 55.4 us -> 60.1 us (1.085)
  the two profiles are of different devices: /device:TPU:0 before, /device:TPU:31 now
where the time goes in v7:
time: 60.1 us; the launch traced here: 59.9 us
  Pallas kernels  59.7 us (99%)
    pallas_call x1, Pallas kernels, transfer(): pl.pallas_call(transfer_kernel, out_shape=(jax.ShapeDtypeStruct((3, 16, 5...  51 us
    pallas_call x1, Pallas kernels, smooth(): pl.pallas_call(smooth_kernel, out_shape=jax.ShapeDtypeStruct((3, 16, 96,...  8.72 us

profile of v7, /device:TPU:31, one launch (start us, length us, event | category | flops | bytes accessed | tf_op | source)
XLA Modules:
  0.0 59.9 jit_solution(11031593143573449552)
XLA Ops:
  0.0 51.0 %shard_map.100 = (f32[3,16,512]{2,1,0:T(8,128)}, f32[2,8,512]{2,1,0:T(8,128)}, f32[2,96,512]{2,1,0:T(8,128)}, f32[2,96,512]{2,1,0:T(8,128)}, f32[2,16,96,512]{3,2,1,0:T(8,128)}) custom-call(f32[3,4096]{1,0:T(4,128)} %disp_hbm.1, s32[64,128]{1,0:T(8,128)} %bitcast.8, s32[4,1024]{1,0:T(4,128)} %slot_hbm.1, f32[3,4,1024]{2,1,0:T(4,128)} %bitcast.6, ...), custom_call_target="tpu_custom_call" | custom-call | tf_op jit(solution)/shard_map/pallas_call | solution.py:628
  51.0 8.7 %shard_map.101 = f32[3,16,96,512]{3,2,1,0:T(8,128)} custom-call(s32[1]{0:T(128)} %bitcast.place_ref, f32[3,16,512]{2,1,0:T(8,128)} %get-tuple-element.10.inter_ref, f32[2,8,512]{2,1,0:T(8,128)} %get-tuple-element.11.edge_ref, f32[2,16,96,512]{3,2,1,0:T(8,128)} %get-tuple-element.12.part_hbm, f32[3,16,96,512]{3,2,1,0:T(8,128)} %mesh_hbm.3, ...), custom_call_target="tpu_custom_call" | custom-call | tf_op jit(solution)/shard_map/pallas_call | solution.py:682

commit v8 on v7

--- a/solution.py
+++ b/solution.py
@@ -460,11 +460,10 @@
             me,
         )
 
-    halo_waits = [send_halo(0)]
     kernel_values(2, left, right, upper, lower)
     kernel_values(3, left, right, upper, lower)
     finish(copies)
-    halo_waits.append(send_halo(1))
+    halo_waits = [send_halo(0), send_halo(1)]
 
     gather_members(landed, slot_ref, member)
     for c in range(4):

time: 60.1 us -> 53.1 us (0.88)
  the two profiles are of different devices: /device:TPU:31 before, /device:TPU:32 now
where the time goes in v8:
time: 53.1 us; the launch traced here: 53 us
  Pallas kernels  52.8 us (99%)
    pallas_call x1, Pallas kernels, transfer(): pl.pallas_call(transfer_kernel, out_shape=(jax.ShapeDtypeStruct((3, 16, 5...  44.1 us
    pallas_call x1, Pallas kernels, smooth(): pl.pallas_call(smooth_kernel, out_shape=jax.ShapeDtypeStruct((3, 16, 96,...  8.72 us

profile of v8, /device:TPU:32, one launch (start us, length us, event | category | flops | bytes accessed | tf_op | source)
XLA Modules:
  0.0 53.0 jit_solution(1685246739877598303)
XLA Ops:
  0.0 44.1 %shard_map.100 = (f32[3,16,512]{2,1,0:T(8,128)}, f32[2,8,512]{2,1,0:T(8,128)}, f32[2,96,512]{2,1,0:T(8,128)}, f32[2,96,512]{2,1,0:T(8,128)}, f32[2,16,96,512]{3,2,1,0:T(8,128)}) custom-call(f32[3,4096]{1,0:T(4,128)} %disp_hbm.1, s32[64,128]{1,0:T(8,128)} %bitcast.8, s32[4,1024]{1,0:T(4,128)} %slot_hbm.1, f32[3,4,1024]{2,1,0:T(4,128)} %bitcast.6, ...), custom_call_target="tpu_custom_call" | custom-call | tf_op jit(solution)/shard_map/pallas_call | solution.py:627
  44.1 8.7 %shard_map.101 = f32[3,16,96,512]{3,2,1,0:T(8,128)} custom-call(s32[1]{0:T(128)} %bitcast.place_ref, f32[3,16,512]{2,1,0:T(8,128)} %get-tuple-element.10.inter_ref, f32[2,8,512]{2,1,0:T(8,128)} %get-tuple-element.11.edge_ref, f32[2,16,96,512]{3,2,1,0:T(8,128)} %get-tuple-element.12.part_hbm, f32[3,16,96,512]{3,2,1,0:T(8,128)} %mesh_hbm.3, ...), custom_call_target="tpu_custom_call" | custom-call | tf_op jit(solution)/shard_map/pallas_call | solution.py:681
